TPU v7x, 128 devices: a whole 4x4x4 slice. The times are simulated.
128 devices in a mesh: row: 4 (over y), col: 32 (over z, x, core).
Axes of the slice: x: 4, y: 4, z: 4, core: 2. Of those that a mesh axis runs over, the one named last changes fastest.
Arguments:
- ladder_amps: bfloat16 [6144, 8192], P('row', 'col'), may hold values from -6 to 6
- ladder_integrals: bfloat16 [8192, 4096], P('row', 'col'), may hold values from -0.0625 to 0.0625
- cycle_amps: bfloat16 [32, 320, 4096], P(None, 'col', 'row'), may hold values from -6 to 6
- cycle_integrals: bfloat16 [20480, 12288], P('row', 'col'), may hold values from -0.0390625 to 0.0390625
- amp_screen: int32 [32, 2], P('row'), may hold values 0 or 1
- integral_screen: int32 [128, 64], P('row', 'col'), may hold values 0 or 1
- occupied_i: float32 [32], P('row'), may hold values from -3 to -0.5
- occupied_j: float32 [192], replicated, may hold values from -3 to -0.5
- virtual_a: float32 [64], P('col'), may hold values from 0.5 to 3
- virtual_b: float32 [64], replicated, may hold values from 0.5 to 3
Outputs:
- update: float32 [6144, 4096], P('row', 'col')
All inputs are finite; a program needn't handle non-finite values. No bound on the sum of `amp_screen` or of `integral_screen` on one device may be relied on, other than what follows from the above.
Results may differ from a plain program's by a relative error of at most 0.0023.
Values may be sent and summed in bfloat16 or wider, within the bound.
A program may use at most 192 MiB of HBM per device.

v0:
```python
import jax
import jax.numpy as jnp
from jax import lax
from jax.sharding import PartitionSpec as P


def per_device(
    ladder_amps,
    ladder_integrals,
    cycle_amps,
    cycle_integrals,
    amp_screen,
    integral_screen,
    occupied_i,
    occupied_j,
    virtual_a,
    virtual_b,
):
    width_tile = virtual_b.shape[0]
    pair_count = occupied_j.shape[0]
    local_i = occupied_i.shape[0]
    col_count = lax.axis_size("col")
    int_mask = jnp.repeat(
        jnp.repeat(integral_screen, width_tile, axis=0), width_tile, axis=1
    ).astype(jnp.bfloat16)
    screened_ints = ladder_integrals * int_mask
    ladder_full, cycle_full = (
        lax.all_gather(screened_ints, "row", axis=0, tiled=True),
        lax.all_gather(cycle_integrals, "row", axis=0, tiled=True),
    )
    panel = lax.all_gather(ladder_amps, "col", axis=1, tiled=True)
    count = panel.shape[1]
    columns = jnp.arange(count, dtype=jnp.int32)
    tiles = columns // (width_tile * width_tile)
    screen = jnp.take(amp_screen, tiles, axis=1)
    screen = jnp.repeat(screen, pair_count, axis=0).astype(jnp.bfloat16)
    integral_rows = ladder_full
    ladder_term = jnp.dot(panel * screen, integral_rows, preferred_element_type=jnp.float32)
    permuted = lax.all_to_all(cycle_amps, "row", split_axis=0, concat_axis=2, tiled=True)
    k_local = permuted.shape[1]
    cycle_cols = permuted.reshape(local_i, k_local, width_tile, width_tile).transpose(0, 2, 1, 3)
    cycle_cols = cycle_cols.reshape(local_i * width_tile, k_local * width_tile)
    integral_rows = cycle_full
    cycle_term = jnp.dot(
        lax.all_gather(cycle_cols, "col", axis=1, tiled=True),
        integral_rows,
        preferred_element_type=jnp.float32,
    )
    cycle_term = cycle_term.astype(jnp.bfloat16)
    j_local = cycle_integrals.shape[1] // width_tile
    cycle_four = cycle_term.reshape(local_i, width_tile, j_local, width_tile)
    returned = lax.all_to_all(cycle_four, "col", split_axis=1, concat_axis=2, tiled=True)
    returned = returned.transpose(0, 2, 1, 3)
    cycle_back = returned.reshape(local_i * pair_count, width_tile // col_count * width_tile)
    residual = ladder_term + cycle_back.astype(jnp.float32)
    virtual_sum = (virtual_a[:, None] + virtual_b[None, :]).reshape(-1)
    occupied_sum = (occupied_i[:, None] + occupied_j[None, :]).reshape(-1)
    denominator = virtual_sum[None, :] - occupied_sum[:, None]
    return residual / denominator


def solution(mesh):
    placed = (
        P("row", "col"),
        P("row", "col"),
        P(None, "col", "row"),
        P("row", "col"),
        P("row", None),
        P("row", "col"),
        P("row"),
        P(),
        P("col"),
        P(),
    )
    return jax.shard_map(
        per_device, mesh=mesh, in_specs=placed, out_specs=P("row", "col"), check_vma=False
    )
```

profile of v0, /device:TPU:7, one launch (start us, length us, event | category | flops | bytes accessed | tf_op | source)
XLA Modules:
  0.0 404.0 jit_solution(17023042232032442343)
XLA Ops:
  6.5 0.7 all-gather.11.cloned.1.call-update
  7.3 0.0 all-gather.9.cloned.1.call-start
  7.3 0.3 copy-done.2
  7.6 0.4 copy.43
  8.0 18.2 %all_to_all.27 = bf16[32,10,1024]{2,1,0:T(8,128)(2,1)S(1)} all-to-all(bf16[32,10,1024]{2,1,0:T(8,128)(2,1)S(1)} %copy.43), channel_id=1, replica_groups=mesh['row'=4,'col'=32] {'row'}, dimensions={0} | all-to-all | bytes 1310720 | tf_op jit(solution)/shard_map/all_to_all | solution.py:39
  26.2 0.5 copy.57
  26.7 0.0 copy-start.3
  26.7 0.0 copy-start.8
  26.8 0.8 reshape.101
  27.5 0.9 copy.45
  28.4 1.6 reshape.102
  30.1 0.0 all-gather.9.cloned.1.call-update
  30.1 0.0 all-gather.5.cloned.1.call-start
  30.1 0.7 all-gather.5.cloned.1.call-update
  30.8 0.0 all-gather.7.cloned.1.call-start
  30.9 0.2 copy.42
  31.1 0.1 broadcast_in_dim.26
  31.2 0.1 convert_element_type.39
  31.3 0.8 bitcast_multiply_fusion.1
  32.2 0.0 all-gather.7.cloned.1.call-update
  32.3 27.8 %gather_fusion = s32[8192,8]{1,0:T(8,128)} fusion(s32[8,2]{0,1:T(2,128)S(1)} %copy-done, s32[8192]{0:T(1024)S(1)} %broadcast_clamp_fusion), kind=kCustom, calls=%fused_computation | custom fusion | bytes 557056 | tf_op jit(solution)/shard_map/jit(_take)/gather | solution.py:35
  60.1 6.0 %fusion.1 = bf16[8,8192]{0,1:T(8,128)(2,1)S(1)} fusion(s32[8192,8]{1,0:T(8,128)} %gather_fusion, pred[8192]{0:T(1024)(128)(4,1)S(1)} %fusion.6), kind=kLoop, calls=%fused_computation.5 | loop fusion | flops 131072 | bytes 401408 | tf_op jit(solution)/shard_map/convert_element_type | solution.py:36
  66.1 0.8 copy.41
  66.9 89.7 %all-gather.11.cloned.1.call-done = bf16[20480,384]{1,0:T(8,128)(2,1)} async-done(((bf16[5120,384]{1,0:T(8,128)(2,1)}), bf16[20480,384]{1,0:T(8,128)(2,1)}) %all-gather.11.cloned.1.call-update) | async-done | bytes 15728656 | tf_op jit(solution)/shard_map/all_gather | solution.py:29
  156.6 86.1 %all-gather.9.cloned.1.call-done = bf16[512,20480]{0,1:T(8,128)(2,1)} async-done(((bf16[512,640]{0,1:T(8,128)(2,1)}), bf16[512,20480]{0,1:T(8,128)(2,1)}) %all-gather.9.cloned.1.call-update) | async-done | bytes 20971536 | tf_op jit(solution)/shard_map/all_gather | solution.py:45
  242.7 17.5 %convolution_convert_fusion = bf16[512,384]{1,0:T(8,128)(2,1)S(1)} fusion(bf16[512,20480]{0,1:T(8,128)(2,1)} %all-gather.9.cloned.1.call-done, bf16[20480,384]{1,0:T(8,128)(2,1)} %all-gather.11.cloned.1.call-done), kind=kOutput, calls=%fused_computation.7 | convolution fusion | flops 8053260288 | bytes 37093376 | tf_op jit(solution)/shard_map/dot_general | solution.py:44
  260.2 0.0 copy-start.4
  260.2 0.0 copy-start.5
  260.2 0.0 copy-start.6
  260.3 0.0 copy-start.7
  260.3 0.6 reshape.115
  260.8 0.9 copy.58
  261.8 1.2 reshape.117
  262.9 5.5 %all-to-all-start.1 = ((bf16[32,2,3072]{2,1,0:T(2,128)(2,1)}), bf16[32,2,3072]{2,1,0:T(2,128)(2,1)S(1)}, u32[]{:S(2)}, u32[]{:S(2)}) async-start(bf16[32,2,3072]{2,1,0:T(2,128)(2,1)} %reshape.117), calls=%async_computation.1 | async-start | bytes 786432 | tf_op jit(solution)/shard_map/all_to_all | solution.py:52
  268.5 0.1 broadcast_add_fusion
  268.6 0.1 add.86
  268.7 0.1 broadcast_add_fusion.1
  268.7 0.1 add.82
  268.8 12.2 %all-to-all-done.1 = bf16[32,2,3072]{2,1,0:T(2,128)(2,1)S(1)} async-done(((bf16[32,2,3072]{2,1,0:T(2,128)(2,1)}), bf16[32,2,3072]{2,1,0:T(2,128)(2,1)S(1)}, u32[]{:S(2)}, u32[]{:S(2)}) %all-to-all-start.1) | async-done | bytes 393248 | tf_op jit(solution)/shard_map/all_to_all | solution.py:52
  281.0 0.5 reshape.118
  281.5 0.2 convert_bitcast_fusion
  281.7 0.1 copy.48
  281.8 1.2 copy.53
  283.0 0.9 reshape.116
  283.9 67.7 %all-gather.5.cloned.1.call-done = bf16[1536,8192]{1,0:T(8,128)(2,1)} async-done(((bf16[1536,256]{1,0:T(8,128)(2,1)}), bf16[1536,8192]{1,0:T(8,128)(2,1)}) %all-gather.5.cloned.1.call-update) | async-done | bytes 25165840 | tf_op jit(solution)/shard_map/all_gather | solution.py:31
  351.5 17.9 %bitcast_multiply_fusion = bf16[1536,8192]{1,0:T(8,128)(2,1)} fusion(bf16[1536,8192]{1,0:T(8,128)(2,1)} %all-gather.5.cloned.1.call-done, bf16[8,8192]{1,0:T(8,128)(2,1)S(1)} %copy.41), kind=kLoop, calls=%fused_computation.1 | loop fusion | flops 12582912 | bytes 50462720 | tf_op jit(solution)/shard_map/mul | solution.py:38
  369.4 15.1 %all-gather.7.cloned.1.call-done = bf16[8192,128]{0,1:T(8,128)(2,1)} async-done(((bf16[2048,128]{0,1:T(8,128)(2,1)}), bf16[8192,128]{0,1:T(8,128)(2,1)}) %all-gather.7.cloned.1.call-update) | async-done | bytes 2097168 | tf_op jit(solution)/shard_map/all_gather | solution.py:28
  384.5 13.0 %fusion = f32[1536,128]{1,0:T(8,128)} fusion(f32[1536,128]{1,0:T(8,128)S(1)} %reshape.116, bf16[1536,8192]{1,0:T(8,128)(2,1)} %bitcast_multiply_fusion, bf16[8192,128]{0,1:T(8,128)(2,1)} %all-gather.7.cloned.1.call-done, f32[1536]{0:T(1024)S(1)} %add.86, f32[128]{0:T(128)S(1)} %add.82), kind=kOutput, calls=%fused_computation.4 | convolution fusion | flops 3221815296 | bytes 28842496 | tf_op jit(solution)/shard_map/dot_general | solution.py:38
  (16 shorter events, 0.1 us)
Async XLA Ops:
  6.5 25.7 %copy-start = (s32[8,2]{0,1:T(2,128)S(1)}, s32[8,2]{0,1:T(2,128)}, u32[]{:S(2)}) copy-start(s32[8,2]{0,1:T(2,128)} %param.14) | copy-start | bytes 196
  6.5 1.1 copy-start.2
  6.5 150.0 %all-gather.11.cloned.1.call-start = ((), (), s32[]{:S(2)}) async-start(), calls=%async_computation.5 | async-start | bytes 19660800 | tf_op jit(solution)/shard_map/all_gather | solution.py:29
  7.3 235.5 %all-gather.9.cloned.1.call-start = ((), (), s32[]{:S(2)}) async-start(), calls=%async_computation.4 | async-start | bytes 21626880 | tf_op jit(solution)/shard_map/all_gather | solution.py:45
  26.7 4.2 %copy-start.3 = (bf16[2048,128]{1,0:T(8,128)(2,1)S(1)}, bf16[2048,128]{1,0:T(8,128)(2,1)}, u32[]{:S(2)}) copy-start(bf16[2048,128]{1,0:T(8,128)(2,1)} %param.11) | copy-start | bytes 1572868
  26.7 4.4 %copy-start.8 = (s32[32,2]{0,1:T(2,128)S(1)}, s32[32,2]{0,1:T(2,128)}, u32[]{:S(2)}) copy-start(s32[32,2]{0,1:T(2,128)} %param.15) | copy-start | bytes 772
  30.1 321.4 %all-gather.5.cloned.1.call-start = ((), (), s32[]{:S(2)}) async-start(), calls=%async_computation.2 | async-start | bytes 25952256 | tf_op jit(solution)/shard_map/all_gather | solution.py:31
  30.8 353.7 %all-gather.7.cloned.1.call-start = ((), (), s32[]{:S(2)}) async-start(), calls=%async_computation.3 | async-start | bytes 2621440 | tf_op jit(solution)/shard_map/all_gather | solution.py:28
  260.2 8.3 %copy-start.4 = (f32[192]{0:T(256)S(1)}, f32[192]{0:T(256)}, u32[]{:S(2)}) copy-start(f32[192]{0:T(256)} %param.17) | copy-start | bytes 2308
  260.2 8.3 %copy-start.5 = (f32[8]{0:T(128)S(1)}, f32[8]{0:T(128)}, u32[]{:S(2)}) copy-start(f32[8]{0:T(128)} %param.16) | copy-start | bytes 100
  260.2 8.4 %copy-start.6 = (f32[64]{0:T(128)S(1)}, f32[64]{0:T(128)}, u32[]{:S(2)}) copy-start(f32[64]{0:T(128)} %param.19) | copy-start | bytes 772
  260.3 8.4 %copy-start.7 = (f32[2]{0:T(128)S(1)}, f32[2]{0:T(128)}, u32[]{:S(2)}) copy-start(f32[2]{0:T(128)} %param.18) | copy-start | bytes 28
  262.9 18.1 %all-to-all-start.1 = ((bf16[32,2,3072]{2,1,0:T(2,128)(2,1)}), bf16[32,2,3072]{2,1,0:T(2,128)(2,1)S(1)}, u32[]{:S(2)}, u32[]{:S(2)}) async-start(bf16[32,2,3072]{2,1,0:T(2,128)(2,1)} %reshape.117), calls=%async_computation.1 | async-start | bytes 786432 | tf_op jit(solution)/shard_map/all_to_all | solution.py:52
  384.5 13.0 %copy-start.1 = (s32[8,2]{0,1:T(2,128)S(1)}, s32[8,2]{0,1:T(2,128)}, u32[]{:S(2)}) copy-start(s32[8,2]{0,1:T(2,128)} %param.14) | copy-start | bytes 196
Sparse Core Ops, SparseCore 0:
  9.0 147.5 all-gather.10
  158.8 83.8 all-gather.8
  244.9 106.5 all-gather.4
  353.1 31.3 all-gather.6
where the time goes:
time: 405 us; the launch traced here: 404 us
  waiting for transfers between devices  272 us (67%)
  local copies, waits for them, and re-layouts  39.1 us (10%)
  matrix products  30.5 us (8%)
  other arithmetic  25.1 us (6%)
  blocking collectives  18.2 us (4%)
  between operations  13.4 us (3%)
  starting transfers between devices  5.65 us (1%)
    all_gather x1, waiting for transfers between devices, per_device(): lax.all_gather(cycle_integrals, 'row', axis=0, tiled=True)  89.7 us
    all_gather x1, waiting for transfers between devices, per_device(): lax.all_gather(cycle_cols, 'col', axis=1, tiled=True)  86.1 us
    all_gather x1, waiting for transfers between devices, per_device(): panel = lax.all_gather(ladder_amps, 'col', axis=1, tiled=True)  67.7 us
    gather x1, local copies, waits for them, and re-layouts, per_device(): screen = jnp.take(amp_screen, tiles, axis=1)  27.8 us
    all_to_all x1, blocking collectives, per_device(): lax.all_to_all(cycle_amps, 'row', split_axis=0, concat_axis=2, tiled=True)  18.2 us
    mul x1, other arithmetic, per_device(): panel * screen  17.9 us
    dot_general x1, matrix products, per_device(): jnp.dot(lax.all_gather(cycle_cols, 'col', axis=1, tiled=True), integral_r...  17.5 us
    all_gather x1, waiting for transfers between devices, per_device(): lax.all_gather(screened_ints, 'row', axis=0, tiled=True)  15.1 us
  transfers between devices with their start and end apart: 5, of which 5 were waited for; matrix products, arithmetic and copies ran while one was open for 20% of the time, Pallas kernels for 0%

commit v1 on v0

v1 whole, which is shorter than its diff:
```python
import functools

import jax
import jax.numpy as jnp
from jax import lax
from jax.experimental import pallas as pl
from jax.experimental.pallas import tpu as pltpu
from jax.sharding import PartitionSpec as P

MESH = pl.DeviceIdType.MESH
N = 4
SENDS = 160


def kernel(
    s_ref,
    la_ref,
    lb_ref,
    cb_ref,
    lad_ref,
    fin_ref,
    a_buf,
    la_buf,
    lb_buf,
    lc,
    lc_a,
    lc_b,
    cc,
    cc_a,
    cc_b,
    outb,
    fin,
    send_sem,
    a_sem,
    la_sem,
    lx_sem,
    lb_sem,
    lc_sem,
    cc_sem,
    fin_sem,
    local_sem,
):
    y = lax.axis_index("row")
    col = lax.axis_index("col")
    z = col // 8
    x = (col // 2) % N
    c = col % 2

    def wrap(value):
        return lax.rem(value + 2 * N, N)

    def device(yy, zz, xx, core):
        return (yy, zz * 8 + xx * 2 + core)

    sibling = device(y, z, x, 1 - c)
    partner = device(z, y, x, c)
    rows, depth = s_ref.shape
    half_rows = rows // 2

    barrier = pltpu.get_barrier_semaphore()

    def greet(other):
        pl.semaphore_signal(barrier, inc=1, device_id=other, device_id_type=MESH)

    for step in range(1, 8 * N):
        greet((y, lax.rem(col + step, 8 * N)))
    for step in range(1, N):
        greet((wrap(y + step), col))

    @pl.when(y != z)
    def _():
        greet(partner)
        pl.semaphore_wait(barrier, 8 * N + N - 1)

    @pl.when(y == z)
    def _():
        pl.semaphore_wait(barrier, 8 * N + N - 2)

    started = []

    def send(src, dst, sem, other):
        copy = pltpu.make_async_remote_copy(
            src_ref=src,
            dst_ref=dst,
            send_sem=send_sem.at[len(started)],
            recv_sem=sem,
            device_id=other,
            device_id_type=MESH,
        )
        copy.start()
        started.append(copy)

    def arrived(dst, sem):
        pltpu.make_async_remote_copy(
            src_ref=dst,
            dst_ref=dst,
            send_sem=send_sem.at[0],
            recv_sem=sem,
            device_id=sibling,
            device_id_type=MESH,
        ).wait_recv()

    def a_slot(p1, p2, h=None):
        zz, xx = c * p1 + (1 - c) * p2, c * p2 + (1 - c) * p1
        if h is None:
            return a_buf.at[zz, xx, c], a_sem.at[zz, xx, c, 0]
        return a_buf.at[zz, xx, c, pl.ds(h * half_rows, half_rows)], a_sem.at[zz, xx, c, h]

    la_half = la_ref.shape[0] // 2

    def la_slot(zz, core, h=None):
        if h is None:
            return la_buf.at[zz, core], la_sem.at[zz, core, 0]
        return la_buf.at[zz, core, pl.ds(h * la_half, la_half)], la_sem.at[zz, core, h]

    lb_rows = lb_buf.shape[1]
    lb_half = lb_rows // 2

    def lb_slot(yy, h):
        return lb_buf.at[yy, pl.ds(h * lb_half, lb_half)], lb_sem.at[yy, h]

    def ring_start(slot, at, plus, minus):
        for h, other in ((0, plus), (1, minus), (1, plus), (0, minus)):
            ref, sem = slot(at, h)
            send(ref, ref, sem, other)

    def ring_near(slot, at, plus, minus):
        ref, sem = slot(wrap(at - 1), 0)
        arrived(ref, sem)
        send(ref, ref, sem, plus)
        ref, sem = slot(wrap(at + 1), 1)
        arrived(ref, sem)
        send(ref, ref, sem, minus)
        arrived(*slot(wrap(at - 1), 1))
        arrived(*slot(wrap(at + 1), 0))

    def ring_far(slot, at):
        for h in range(2):
            arrived(*slot(wrap(at + 2), h))

    def share(ref, sem):
        send(ref, ref, sem, sibling)

    p1, p2 = c * z + (1 - c) * x, c * x + (1 - c) * z
    d1_plus = device(y, wrap(z + c), wrap(x + 1 - c), c)
    d1_minus = device(y, wrap(z - c), wrap(x - 1 + c), c)
    d2_plus = device(y, wrap(z + 1 - c), wrap(x + c), c)
    d2_minus = device(y, wrap(z - 1 + c), wrap(x - c), c)
    z_plus, z_minus = device(y, wrap(z + 1), x, c), device(y, wrap(z - 1), x, c)
    x_plus, x_minus = device(y, z, wrap(x + 1), c), device(y, z, wrap(x - 1), c)
    y_plus, y_minus = (wrap(y + 1), col), (wrap(y - 1), col)

    def own_block(h):
        part = pl.ds(h * half_rows, half_rows)
        return s_ref.at[part], a_buf.at[y, x, c, part], a_sem.at[y, x, c, h]

    @pl.when(y != z)
    def _():
        for h in range(2):
            src, dst, sem = own_block(h)
            pltpu.make_async_remote_copy(
                src_ref=src,
                dst_ref=dst,
                send_sem=send_sem.at[SENDS - 1 - h],
                recv_sem=sem,
                device_id=partner,
                device_id_type=MESH,
            ).start()

    @pl.when(y == z)
    def _():
        a_buf[z, x, c] = s_ref[...]

    width = lb_ref.shape[1]
    for step in range(1, N):
        to = wrap(x + step)
        send(
            lb_ref.at[pl.ds(pl.multiple_of(to * lb_rows, lb_rows), lb_rows)],
            lb_buf.at[y, :, pl.ds(pl.multiple_of(x * width, width), width)],
            lx_sem.at[x],
            device(y, z, to, c),
        )
    keep_lb = pltpu.make_async_copy(
        lb_ref.at[pl.ds(pl.multiple_of(x * lb_rows, lb_rows), lb_rows)],
        lb_buf.at[y, :, pl.ds(pl.multiple_of(x * width, width), width)],
        local_sem.at[0],
    )
    keep_lb.start()
    keep_la = pltpu.make_async_copy(la_ref, la_buf.at[z, c], local_sem.at[1])
    keep_la.start()
    keep_la.wait()
    ring_start(lambda p, h: la_slot(p, c, h), z, z_plus, z_minus)
    share(*la_slot(z, c))

    @pl.when(y != z)
    def _():
        for h in range(2):
            src, _, _ = own_block(h)
            dst, sem = a_buf.at[z, x, c, pl.ds(h * half_rows, half_rows)], a_sem.at[z, x, c, h]
            copy = pltpu.make_async_remote_copy(
                src_ref=src,
                dst_ref=dst,
                send_sem=send_sem.at[SENDS - 1 - h],
                recv_sem=sem,
                device_id=partner,
                device_id_type=MESH,
            )
            copy.wait_send()
            copy.wait_recv()

    def first(p, h=None):
        return a_slot(p, p2, h)

    def second(q):
        return lambda p, h=None: a_slot(q, p, h)

    ring_start(first, p1, d1_plus, d1_minus)
    ring_start(second(p1), p2, d2_plus, d2_minus)
    share(*a_slot(p1, p2))

    keep_lb.wait()
    for step in range(1, N):
        source = wrap(x + step)
        arrived(lb_buf.at[y, :, pl.ds(pl.multiple_of(source * width, width), width)], lx_sem.at[source])
    ring_start(lb_slot, y, y_plus, y_minus)

    ring_near(first, p1, d1_plus, d1_minus)
    for q in (wrap(p1 - 1), wrap(p1 + 1)):
        ring_start(second(q), p2, d2_plus, d2_minus)
        share(*a_slot(q, p2))

    ring_near(lambda p, h: la_slot(p, c, h), z, z_plus, z_minus)
    for q in (wrap(z - 1), wrap(z + 1)):
        share(*la_slot(q, c))
    ring_near(lb_slot, y, y_plus, y_minus)

    ring_far(first, p1)
    q = wrap(p1 + 2)
    ring_start(second(q), p2, d2_plus, d2_minus)
    share(*a_slot(q, p2))

    def second_near(q):
        ring_near(second(q), p2, d2_plus, d2_minus)
        for p in (wrap(p2 - 1), wrap(p2 + 1)):
            share(*a_slot(q, p))

    def second_far(q):
        ring_far(second(q), p2)
        share(*a_slot(q, wrap(p2 + 2)))

    second_near(p1)

    ring_far(lambda p, h: la_slot(p, c, h), z)
    share(*la_slot(wrap(z + 2), c))
    ring_far(lb_slot, y)
    for step in range(N):
        arrived(*la_slot(wrap(z + step), 1 - c))

    tile = 256
    lk = la_ref.shape[1]

    @pl.loop(0, la_ref.shape[0] // tile)
    def _(m):
        part = pl.ds(pl.multiple_of(m * tile, tile), tile)
        total = jnp.zeros((tile, lb_buf.shape[2]), jnp.float32)
        for zz in range(N):
            for core in range(2):
                total += jnp.dot(
                    la_buf[zz, core, part, :],
                    lb_buf[zz, pl.ds(core * lk, lk), :],
                    preferred_element_type=jnp.float32,
                )
        for xx in range(N):
            lc[xx, part, :] = total[:, xx * width : (xx + 1) * width]

    def reduce_start(ref, land, sem, at, plus, minus):
        half = ref.shape[1] // 2
        for h, other in ((0, plus), (1, minus)):
            send(ref.at[wrap(at + 2), pl.ds(h * half, half)], land.at[h], sem.at[h], other)

    def reduce_middle(ref, land_a, land_b, sem, at, plus, minus):
        half = ref.shape[1] // 2
        for h, to, other in ((0, wrap(at + 1), plus), (1, wrap(at - 1), minus)):
            arrived(land_a.at[h], sem.at[h])
            part = pl.ds(h * half, half)
            ref[to, part, :] = ref[to, part, :] + land_a[h]
            send(ref.at[to], land_b.at[h], sem.at[2 + h], other)

    def reduce_end(ref, land_b, sem, at):
        for h in range(2):
            arrived(land_b.at[h], sem.at[2 + h])
        return ref[at] + land_b[0] + land_b[1]

    reduce_start(lc, lc_a, lc_sem, x, x_plus, x_minus)

    second_far(p1)
    second_near(wrap(p1 - 1))
    reduce_middle(lc, lc_a, lc_b, lc_sem, x, x_plus, x_minus)
    second_near(wrap(p1 + 1))
    second_near(wrap(p1 + 2))
    second_far(wrap(p1 - 1))
    second_far(wrap(p1 + 1))
    second_far(wrap(p1 + 2))

    lad_ref[...] = reduce_end(lc, lc_b, lc_sem, x)

    offsets = (0, 1, 3, 2)

    def block(k):
        zz = wrap(z + offsets[k])
        for xx in range(N):
            arrived(a_buf.at[zz, xx, 1 - c], a_sem.at[zz, xx, 1 - c, 0])

        @pl.loop(0, rows // tile)
        def _(m):
            part = pl.ds(pl.multiple_of(m * tile, tile), tile)
            total = jnp.zeros((tile, cb_ref.shape[1]), jnp.float32)
            for xx in range(N):
                for core in range(2):
                    total += jnp.dot(
                        a_buf[zz, xx, core, part, :],
                        cb_ref[pl.ds((xx * 2 + core) * depth, depth), :],
                        preferred_element_type=jnp.float32,
                    )
            quarter = rows // N
            for n in range(tile // quarter):
                cc[k, m * (tile // quarter) + n] = total[n * quarter : (n + 1) * quarter]

        reduce_start(cc.at[k], cc_a.at[k], cc_sem.at[k], y, y_plus, y_minus)

    def block_middle(k):
        reduce_middle(cc.at[k], cc_a.at[k], cc_b.at[k], cc_sem.at[k], y, y_plus, y_minus)

    piece = rows // N // 8

    def block_end(k):
        total = reduce_end(cc.at[k], cc_b.at[k], cc_sem.at[k], y)
        outb[k] = total.astype(outb.dtype)
        zz = wrap(z + offsets[k])
        mine = x * 2 + c
        for step in range(1 if k == 0 else 0, 8):
            to = lax.rem(mine + step, 8)
            send(
                outb.at[k, pl.ds(pl.multiple_of(to * piece, piece), piece)],
                fin.at[col],
                fin_sem.at[col],
                (y, zz * 8 + to),
            )
        if k == 0:
            fin[col] = outb[k, pl.ds(pl.multiple_of(mine * piece, piece), piece), :]

    block(0)
    block(1)
    block_middle(0)
    block(2)
    block_middle(1)
    block_end(0)
    block(3)
    block_middle(2)
    block_end(1)
    block_middle(3)
    block_end(2)
    block_end(3)

    for step in range(1, 8 * N):
        source = lax.rem(col + step, 8 * N)
        arrived(fin.at[source], fin_sem.at[source])
    fin_ref[...] = fin[...]
    for copy in started:
        copy.wait_send()


def per_device(
    ladder_amps,
    ladder_integrals,
    cycle_amps,
    cycle_integrals,
    amp_screen,
    integral_screen,
    occupied_i,
    occupied_j,
    virtual_a,
    virtual_b,
):
    tile = virtual_b.shape[0]
    pair_count = occupied_j.shape[0]
    local_i = occupied_i.shape[0]
    local_a = virtual_a.shape[0]
    col = lax.axis_index("col")
    col_count = lax.axis_size("col")

    local_cols = ladder_amps.shape[1]
    mine = lax.dynamic_slice_in_dim(amp_screen, (col * local_cols) // (tile * tile), 1, axis=1)
    amp_mask = jnp.broadcast_to(mine[:, None, :], (local_i, pair_count, 1)).reshape(-1, 1)
    la = ladder_amps * amp_mask.astype(jnp.bfloat16)
    int_mask = jnp.repeat(jnp.repeat(integral_screen, tile, axis=0), tile, axis=1).astype(jnp.bfloat16)
    lb = ladder_integrals * int_mask

    all_i, local_k, _ = cycle_amps.shape
    s = cycle_amps.reshape(N, all_i // N, local_k, 8, local_a, tile).transpose(0, 3, 1, 4, 2, 5)
    s = s.reshape(all_i * 8 * local_a, local_k * tile)

    rows, depth = s.shape
    nc = cycle_integrals.shape[1]
    lm, lk = la.shape
    lrows, ln = lb.shape
    quarter = rows // N
    piece = quarter // 8
    f32, bf16 = jnp.float32, jnp.bfloat16
    dma = pltpu.SemaphoreType.DMA
    vmem = pl.BlockSpec(memory_space=pltpu.VMEM)
    ladder, cycle = pl.pallas_call(
        kernel,
        out_shape=(
            jax.ShapeDtypeStruct((lm, ln), f32),
            jax.ShapeDtypeStruct((col_count, piece, nc), bf16),
        ),
        in_specs=[vmem] * 4,
        out_specs=(vmem, vmem),
        scratch_shapes=[
            pltpu.VMEM((N, N, 2, rows, depth), bf16),
            pltpu.VMEM((N, 2, lm, lk), bf16),
            pltpu.VMEM((N, lrows // N, N * ln), bf16),
            pltpu.VMEM((N, lm, ln), f32),
            pltpu.VMEM((2, lm // 2, ln), f32),
            pltpu.VMEM((2, lm, ln), f32),
            pltpu.VMEM((N, N, quarter, nc), f32),
            pltpu.VMEM((N, 2, quarter // 2, nc), f32),
            pltpu.VMEM((N, 2, quarter, nc), f32),
            pltpu.VMEM((N, quarter, nc), bf16),
            pltpu.VMEM((col_count, piece, nc), bf16),
            dma((SENDS,)),
            dma((N, N, 2, 2)),
            dma((N, 2, 2)),
            dma((N,)),
            dma((N, 2)),
            dma((4,)),
            dma((N, 4)),
            dma((col_count,)),
            dma((2,)),
        ],
        compiler_params=pltpu.CompilerParams(
            collective_id=0, has_side_effects=True, vmem_limit_bytes=56 * 2**20
        ),
        cost_estimate=pl.CostEstimate(
            flops=2 * (N * rows * N * 2 * depth * nc + lm * N * 2 * lk * N * ln),
            bytes_accessed=8 * 2**20,
            transcendentals=0,
        ),
    )(s, la, lb, cycle_integrals)

    j_local = nc // tile
    cycle = cycle.reshape(col_count, local_i, local_a, j_local, tile).transpose(1, 0, 3, 2, 4)
    cycle = cycle.reshape(local_i * pair_count, local_a * tile)
    residual = ladder + cycle.astype(f32)
    virtual_sum = (virtual_a[:, None] + virtual_b[None, :]).reshape(-1)
    occupied_sum = (occupied_i[:, None] + occupied_j[None, :]).reshape(-1)
    denominator = virtual_sum[None, :] - occupied_sum[:, None]
    return residual / denominator


def solution(mesh):
    placed = (
        P("row", "col"),
        P("row", "col"),
        P(None, "col", "row"),
        P("row", "col"),
        P("row", None),
        P("row", "col"),
        P("row"),
        P(),
        P("col"),
        P(),
    )
    return jax.shard_map(
        per_device, mesh=mesh, in_specs=placed, out_specs=P("row", "col"), check_vma=False
    )
```

time: 405 us -> 195 us (0.48)
  waiting for transfers between devices: 272 us -> 0 us
  Pallas kernels: 0 us -> 176 us
  matrix products: 30.5 us -> 0 us
  local copies, waits for them, and re-layouts: 39.1 us -> 13.4 us
  other arithmetic: 25.1 us -> 3.41 us
  blocking collectives: 18.2 us -> 0 us
  between operations: 13.4 us -> 0.13 us
  starting transfers between devices: 5.65 us -> 0 us
    all_gather x4 -> x0, waiting for transfers between devices: 259 us -> none  [the longest x1 89.7 us: per_device(): lax.all_gather(cycle_integrals, 'row', axis=0, tiled=True)]
    pallas_call x0 -> x1, Pallas kernels: none -> 176 us  [per_device(): pl.pallas_call(kernel, out_shape=(jax.ShapeDtypeStruct((lm, ln), f32), ja...]
    dot_general x2 -> x0, matrix products: 30.5 us -> none  [the longest x1 17.5 us: per_device(): jnp.dot(lax.all_gather(cycle_cols, 'col', axis=1, tiled=True), integral_r...]
    gather x1 -> x0, local copies, waits for them, and re-layouts: 27.8 us -> none  [per_device(): screen = jnp.take(amp_screen, tiles, axis=1)]
    all_to_all x1 -> x0, blocking collectives: 18.2 us -> none  [per_device(): lax.all_to_all(cycle_amps, 'row', split_axis=0, concat_axis=2, tiled=True)]
    mul x2, other arithmetic: 18.7 us -> 2.1 us  [the longest x1 1.15 us: per_device(): la = ladder_amps * amp_mask.astype(jnp.bfloat16)]
    all_to_all x1 -> x0, waiting for transfers between devices: 12.2 us -> none  [per_device(): lax.all_to_all(cycle_four, 'col', split_axis=1, concat_axis=2, tiled=True)]
    convert_element_type x3 -> x2, other arithmetic: 6.18 us -> 0.01 us  [the longest x1 0.01 us: per_device(): la = ladder_amps * amp_mask.astype(jnp.bfloat16)]
  transfers between devices with their start and end apart: 5 -> 0, of which waited for: 5 -> 0; matrix products, arithmetic and copies ran while one was open for 20% -> 0% of each run, Pallas kernels for 0% -> 0%
where the time goes in v1:
time: 195 us; the launch traced here: 193 us
  Pallas kernels  176 us (90%)
  local copies, waits for them, and re-layouts  13.4 us (7%)
  other arithmetic  3.41 us (2%)
    pallas_call x1, Pallas kernels, per_device(): pl.pallas_call(kernel, out_shape=(jax.ShapeDtypeStruct((lm, ln), f32), ja...  176 us
    convert_element_type x3, local copies, waits for them, and re-layouts, per_device(): residual = ladder + cycle.astype(f32)  5.88 us
    reshape x2, local copies, waits for them, and re-layouts, per_device(): cycle_amps.reshape(N, all_i // N, local_k, 8, local_a, tile)  4.76 us

profile of v1, /device:TPU:7, one launch (start us, length us, event | category | flops | bytes accessed | tf_op | source)
XLA Modules:
  0.0 192.9 jit_solution(13471744735620604965)
XLA Ops:
  0.0 3.1 %reshape.64 = bf16[4,8,10,8,2,64]{5,4,3,1,0,2:T(2,128)(2,1)S(1)} reshape(bf16[32,10,1024]{2,0,1:T(8,128)(2,1)} %param.12) | data formatting | bytes 1310720 | tf_op jit(solution)/shard_map/reshape | solution.py:400
  3.2 1.6 copy.18
  4.8 0.0 copy-start.7
  4.8 0.0 copy-start
  4.8 0.0 copy-start.8
  4.8 1.9 reshape.65.s_ref
  6.7 0.0 copy-start.2
  6.7 0.0 copy-done.7
  6.7 0.1 broadcast_in_dim.6
  6.8 0.1 convert_element_type.40
  6.9 0.0 copy-done
  6.9 1.2 broadcast_multiply_fusion.la_ref
  8.0 0.0 copy-done.8
  8.0 0.1 broadcast_in_dim.7
  8.1 0.1 convert_element_type.42
  8.2 0.1 broadcast_in_dim.8
  8.3 0.3 copy.15
  8.5 0.0 copy-done.2
  8.6 0.9 mul.17.lb_ref
  9.5 175.9 %shard_map.100 = (f32[1536,128]{1,0:T(8,128)}, bf16[32,16,384]{2,1,0:T(8,128)(2,1)}) custom-call(bf16[512,640]{1,0:T(8,128)(2,1)} %reshape.65.s_ref, bf16[1536,256]{1,0:T(8,128)(2,1)} %broadcast_multiply_fusion.la_ref, bf16[2048,128]{1,0:T(8,128)(2,1)} %mul.17.lb_ref, bf16[5120,384]{1,0:T(8,128)(2,1)} %cb_ref.1), custom_call_target="tpu_custom_call" | custom-call | flops 11274289152 | bytes 8388608 | tf_op jit(solution)/shard_map/pallas_call | solution.py:412
  185.4 1.5 reshape.67
  187.0 2.0 %copy.16 = f32[8,32,6,2,64]{4,3,2,1,0:T(2,128)} copy(f32[8,32,6,2,64]{4,2,3,0,1:T(8,128)S(1)} %bitcast.11) | data formatting | bytes 1572864 | tf_op jit(solution)/shard_map/convert_element_type | solution.py:455
  188.9 0.0 copy-start.3
  188.9 0.0 copy-start.4
  188.9 0.0 copy-start.5
  188.9 0.0 copy-start.6
  188.9 0.0 copy-start.1
  188.9 2.4 %reshape.66 = f32[1536,128]{1,0:T(8,128)S(1)} reshape(f32[8,32,6,2,64]{4,3,2,1,0:T(2,128)} %copy.16) | data formatting | bytes 1572864 | tf_op jit(solution)/shard_map/convert_element_type | solution.py:455
  191.4 0.0 copy-done.3
  191.4 0.0 copy-done.4
  191.4 0.1 broadcast_add_fusion
  191.5 0.1 add.56
  191.5 0.0 copy-done.5
  191.5 0.0 copy-done.6
  191.5 0.1 broadcast_add_fusion.1
  191.6 0.1 add.52
  191.7 0.0 copy-done.1
  191.7 1.2 subtract_divide_fusion
  (2 shorter events, 0.0 us)
Async XLA Ops:
  4.8 1.9 copy-start.7
  4.8 2.1 %copy-start = (bf16[1536,256]{1,0:T(8,128)(2,1)S(1)}, bf16[1536,256]{1,0:T(8,128)(2,1)}, u32[]{:S(2)}) copy-start(bf16[1536,256]{1,0:T(8,128)(2,1)} %param.10) | copy-start | bytes 2359300
  4.8 3.2 %copy-start.8 = (s32[32,2]{0,1:T(2,128)S(1)}, s32[32,2]{0,1:T(2,128)}, u32[]{:S(2)}) copy-start(s32[32,2]{0,1:T(2,128)} %param.15) | copy-start | bytes 772
  6.7 1.9 copy-start.2
  188.9 2.4 %copy-start.3 = (f32[192]{0:T(256)S(1)}, f32[192]{0:T(256)}, u32[]{:S(2)}) copy-start(f32[192]{0:T(256)} %param.17) | copy-start | bytes 2308
  188.9 2.4 %copy-start.4 = (f32[8]{0:T(128)S(1)}, f32[8]{0:T(128)}, u32[]{:S(2)}) copy-start(f32[8]{0:T(128)} %param.16) | copy-start | bytes 100
  188.9 2.6 %copy-start.5 = (f32[64]{0:T(128)S(1)}, f32[64]{0:T(128)}, u32[]{:S(2)}) copy-start(f32[64]{0:T(128)} %param.19) | copy-start | bytes 772
  188.9 2.6 %copy-start.6 = (f32[2]{0:T(128)S(1)}, f32[2]{0:T(128)}, u32[]{:S(2)}) copy-start(f32[2]{0:T(128)} %param.18) | copy-start | bytes 28
  188.9 2.8 %copy-start.1 = (f32[1536,128]{1,0:T(8,128)S(1)}, f32[1536,128]{1,0:T(8,128)}, u32[]{:S(2)}) copy-start(f32[1536,128]{1,0:T(8,128)} %get-tuple-element.7) | copy-start | bytes 2359300

commit v2 on v1

v2 whole, which is shorter than its diff:
```python
import functools

import jax
import jax.numpy as jnp
from jax import lax
from jax.experimental import pallas as pl
from jax.experimental.pallas import tpu as pltpu
from jax.sharding import PartitionSpec as P

MESH = pl.DeviceIdType.MESH
N = 4
SENDS = 280
GROUPS = 4


def axis_order(core):
    return (core, core, core, core)


def kernel(
    s_ref,
    la_ref,
    lb_ref,
    cb_ref,
    lad_ref,
    fin_ref,
    middle,
    a_buf,
    la_buf,
    lb_buf,
    lc,
    lc_a,
    lc_b,
    cc,
    cc_a,
    cc_b,
    outb,
    fin,
    send_sem,
    middle_sem,
    a_sem,
    la_sem,
    lx_sem,
    lb_sem,
    lc_sem,
    cc_sem,
    fin_sem,
    local_sem,
):
    y = lax.axis_index("row")
    col = lax.axis_index("col")
    z = col // 8
    x = (col // 2) % N
    c = col % 2

    def wrap(value):
        return lax.rem(value + 2 * N, N)

    def device(yy, zz, xx, core):
        return (yy, zz * 8 + xx * 2 + core)

    sibling = device(y, z, x, 1 - c)
    rows, depth = s_ref.shape
    group = rows // GROUPS
    half = group // 2

    barrier = pltpu.get_barrier_semaphore()

    def greet(other):
        pl.semaphore_signal(barrier, inc=1, device_id=other, device_id_type=MESH)

    for step in range(1, 8 * N):
        greet((y, lax.rem(col + step, 8 * N)))
    for step in range(1, N):
        greet((wrap(y + step), col))

    pl.semaphore_wait(barrier, 8 * N + N - 2)

    started = []

    def send(src, dst, sem, other):
        copy = pltpu.make_async_remote_copy(
            src_ref=src,
            dst_ref=dst,
            send_sem=send_sem.at[len(started)],
            recv_sem=sem,
            device_id=other,
            device_id_type=MESH,
        )
        copy.start()
        started.append(copy)

    def arrived(dst, sem):
        pltpu.make_async_remote_copy(
            src_ref=dst,
            dst_ref=dst,
            send_sem=send_sem.at[0],
            recv_sem=sem,
            device_id=sibling,
            device_id_type=MESH,
        ).wait_recv()

    def a_slot(zz, xx, g, h=None):
        if h is None:
            return a_buf.at[zz, xx, c, pl.ds(g * group, group)], a_sem.at[zz, xx, c, g, 0]
        return a_buf.at[zz, xx, c, pl.ds(g * group + h * half, half)], a_sem.at[zz, xx, c, g, h]

    la_half = la_ref.shape[0] // 2

    def la_slot(zz, core, h=None):
        if h is None:
            return la_buf.at[zz, core], la_sem.at[zz, core, 0]
        return la_buf.at[zz, core, pl.ds(h * la_half, la_half)], la_sem.at[zz, core, h]

    lb_rows = lb_buf.shape[1]
    lb_half = lb_rows // 2

    def lb_slot(yy, h):
        return lb_buf.at[yy, pl.ds(h * lb_half, lb_half)], lb_sem.at[yy, h]

    def ring_start(slot, at, plus, minus):
        for h, other in ((0, plus), (1, minus), (1, plus), (0, minus)):
            ref, sem = slot(at, h)
            send(ref, ref, sem, other)

    def ring_near(slot, at, plus, minus):
        ref, sem = slot(wrap(at - 1), 0)
        arrived(ref, sem)
        send(ref, ref, sem, plus)
        ref, sem = slot(wrap(at + 1), 1)
        arrived(ref, sem)
        send(ref, ref, sem, minus)
        arrived(*slot(wrap(at - 1), 1))
        arrived(*slot(wrap(at + 1), 0))

    def ring_far(slot, at):
        for h in range(2):
            arrived(*slot(wrap(at + 2), h))

    def share(ref, sem):
        send(ref, ref, sem, sibling)

    z_plus, z_minus = device(y, wrap(z + 1), x, c), device(y, wrap(z - 1), x, c)
    x_plus, x_minus = device(y, z, wrap(x + 1), c), device(y, z, wrap(x - 1), c)
    y_plus, y_minus = (wrap(y + 1), col), (wrap(y - 1), col)

    def swapped(g, along=None):
        along = z if along is None else along
        return (y + along) % 2 + 2 * ((y // 2 + along // 2 + g % 2) % 2)

    def group_rows(g):
        return pl.ds(g * group, group)

    def over_z(g):
        part = group_rows(g)
        return pltpu.make_async_remote_copy(
            src_ref=s_ref.at[part],
            dst_ref=middle.at[part],
            send_sem=send_sem.at[SENDS - 1 - g],
            recv_sem=middle_sem.at[g],
            device_id=device(y, swapped(g), x, c),
            device_id_type=MESH,
        )

    def over_y(g, ref):
        part = group_rows(g)
        return pltpu.make_async_remote_copy(
            src_ref=ref.at[part],
            dst_ref=a_buf.at[z, x, c, part],
            send_sem=send_sem.at[SENDS - 1 - GROUPS - g],
            recv_sem=a_sem.at[z, x, c, g, 0],
            device_id=(swapped(g), col),
            device_id_type=MESH,
        )

    def start_over_z(g):
        @pl.when(y != 2 * (g % 2))
        def _():
            over_z(g).start()

    def start_over_y(g):
        still = 2 * (g % 2)

        @pl.when(y != still)
        def _():
            over_z(g).wait_recv()

            @pl.when(z != still)
            def _():
                over_y(g, middle).start()

            @pl.when(z == still)
            def _():
                a_buf[z, x, c, group_rows(g), :] = middle[group_rows(g), :]

        @pl.when(y == still)
        def _():
            @pl.when(z != still)
            def _():
                over_y(g, s_ref).start()

            @pl.when(z == still)
            def _():
                a_buf[z, x, c, group_rows(g), :] = s_ref[group_rows(g), :]

    def end_over_y(g):
        @pl.when(z != 2 * (g % 2))
        def _():
            over_y(g, middle).wait_recv()

    width = lb_ref.shape[1]
    for step in range(1, N):
        to = wrap(x + step)
        send(
            lb_ref.at[pl.ds(pl.multiple_of(to * lb_rows, lb_rows), lb_rows)],
            lb_buf.at[y, :, pl.ds(pl.multiple_of(x * width, width), width)],
            lx_sem.at[x],
            device(y, z, to, c),
        )
    keep_lb = pltpu.make_async_copy(
        lb_ref.at[pl.ds(pl.multiple_of(x * lb_rows, lb_rows), lb_rows)],
        lb_buf.at[y, :, pl.ds(pl.multiple_of(x * width, width), width)],
        local_sem.at[0],
    )
    keep_lb.start()
    keep_la = pltpu.make_async_copy(la_ref, la_buf.at[z, c], local_sem.at[1])
    keep_la.start()

    def la_own(p, h=None):
        return la_slot(p, c, h)

    def la_start():
        keep_la.wait()
        ring_start(la_own, z, z_plus, z_minus)
        share(*la_slot(z, c))

    def la_near():
        ring_near(la_own, z, z_plus, z_minus)
        for q in (wrap(z - 1), wrap(z + 1)):
            share(*la_slot(q, c))

    def la_far():
        ring_far(la_own, z)
        share(*la_slot(wrap(z + 2), c))

    def lb_start():
        keep_lb.wait()
        for step in range(1, N):
            source = wrap(x + step)
            arrived(lb_buf.at[y, :, pl.ds(pl.multiple_of(source * width, width), width)], lx_sem.at[source])
        ring_start(lb_slot, y, y_plus, y_minus)

    def lb_near():
        ring_near(lb_slot, y, y_plus, y_minus)

    def lb_far():
        ring_far(lb_slot, y)

    z_first = axis_order(c)

    def ring_of(is_z):
        dz, dx = is_z, 1 - is_z
        plus = device(y, wrap(z + dz), wrap(x + dx), c)
        minus = device(y, wrap(z - dz), wrap(x - dx), c)
        return is_z * z + (1 - is_z) * x, plus, minus

    def first(g):
        f = z_first[g]
        return (lambda q, h=None: a_slot(f * q + (1 - f) * z, f * x + (1 - f) * q, g, h)), ring_of(f)

    def second(g, k):
        f = z_first[g]
        p = wrap(f * z + (1 - f) * x + (0, 3, 1, 2)[k])
        return (lambda q, h=None: a_slot(f * p + (1 - f) * q, f * q + (1 - f) * p, g, h)), ring_of(1 - f)

    def second_start(g, k):
        slot, ring = second(g, k)
        ring_start(slot, *ring)
        share(*slot(ring[0]))

    def second_near(g, k):
        slot, ring = second(g, k)
        ring_near(slot, *ring)
        for p in (wrap(ring[0] - 1), wrap(ring[0] + 1)):
            share(*slot(p))

    def second_far(g, k):
        slot, ring = second(g, k)
        ring_far(slot, ring[0])
        share(*slot(wrap(ring[0] + 2)))

    def first_start(g):
        end_over_y(g)
        slot, ring = first(g)
        ring_start(slot, *ring)
        second_start(g, 0)

    def first_near(g):
        slot, ring = first(g)
        ring_near(slot, *ring)
        second_start(g, 1)
        second_start(g, 2)

    def first_far(g):
        slot, ring = first(g)
        ring_far(slot, ring[0])
        second_start(g, 3)

    def seconds_near(g):
        for k in range(N):
            second_near(g, k)

    def seconds_far(g):
        for k in range(N):
            second_far(g, k)

    tile = 256
    lk = la_ref.shape[1]

    def ladder():
        for step in range(N):
            arrived(*la_slot(wrap(z + step), 1 - c))

        @pl.loop(0, la_ref.shape[0] // tile)
        def _(m):
            part = pl.ds(pl.multiple_of(m * tile, tile), tile)
            total = jnp.zeros((tile, lb_buf.shape[2]), jnp.float32)
            for zz in range(N):
                for core in range(2):
                    total += jnp.dot(
                        la_buf[zz, core, part, :],
                        lb_buf[zz, pl.ds(core * lk, lk), :],
                        preferred_element_type=jnp.float32,
                    )
            for xx in range(N):
                lc[xx, part, :] = total[:, xx * width : (xx + 1) * width]

        reduce_start(lc, lc_a, lc_sem, x, x_plus, x_minus)

    def ladder_middle():
        reduce_middle(lc, lc_a, lc_b, lc_sem, x, x_plus, x_minus)

    def ladder_end():
        lad_ref[...] = reduce_end(lc, lc_b, lc_sem, x)

    def reduce_start(ref, land, sem, at, plus, minus):
        size = ref.shape[1] // 2
        for h, other in ((0, plus), (1, minus)):
            send(ref.at[wrap(at + 2), pl.ds(h * size, size)], land.at[h], sem.at[h], other)

    def reduce_middle(ref, land_a, land_b, sem, at, plus, minus):
        size = ref.shape[1] // 2
        for h, to, other in ((0, wrap(at + 1), plus), (1, wrap(at - 1), minus)):
            arrived(land_a.at[h], sem.at[h])
            part = pl.ds(h * size, size)
            ref[to, part, :] = ref[to, part, :] + land_a[h]
            send(ref.at[to], land_b.at[h], sem.at[2 + h], other)

    def reduce_end(ref, land_b, sem, at):
        for h in range(2):
            arrived(land_b.at[h], sem.at[2 + h])
        return ref[at] + land_b[0] + land_b[1]

    quarter = group // N
    pairs = 8 // GROUPS
    piece = quarter // pairs
    mine = x * 2 + c

    def cycle(g):
        for zz in range(N):
            for xx in range(N):
                arrived(a_buf.at[zz, xx, 1 - c, group_rows(g)], a_sem.at[zz, xx, 1 - c, g, 0])
        total = jnp.zeros((rows // GROUPS * N, cb_ref.shape[1]), jnp.float32)
        for xx in range(N):
            for core in range(2):
                left = jnp.concatenate([a_buf[zz, xx, core, group_rows(g), :] for zz in range(N)], axis=0)
                total += jnp.dot(
                    left,
                    cb_ref[pl.ds((xx * 2 + core) * depth, depth), :],
                    preferred_element_type=jnp.float32,
                )
        for zz in range(N):
            owner = swapped(g, zz)
            for n in range(N):
                cc[g, n, owner] = total[zz * group + n * quarter : zz * group + (n + 1) * quarter]
        reduce_start(cc.at[g], cc_a.at[g], cc_sem.at[g], y, y_plus, y_minus)

    def cycle_middle(g):
        reduce_middle(cc.at[g], cc_a.at[g], cc_b.at[g], cc_sem.at[g], y, y_plus, y_minus)

    def last_copy(g):
        turn = lax.rem(mine, pairs)
        return pltpu.make_async_remote_copy(
            src_ref=outb.at[g, z, pl.ds(pl.multiple_of(turn * piece, piece), piece)],
            dst_ref=fin.at[col],
            send_sem=send_sem.at[SENDS - 1 - 2 * GROUPS - g],
            recv_sem=fin_sem.at[col],
            device_id=(y, z * 8 + g * pairs + turn),
            device_id_type=MESH,
        )

    def cycle_end(g):
        outb[g] = reduce_end(cc.at[g], cc_b.at[g], cc_sem.at[g], y).astype(outb.dtype)
        for zstep in range(N):
            zz = wrap(z + zstep)
            for step in range(pairs):
                if zstep == 0 and step == 0:
                    continue
                turn = lax.rem(mine + step, pairs)
                send(
                    outb.at[g, zz, pl.ds(pl.multiple_of(turn * piece, piece), piece)],
                    fin.at[col],
                    fin_sem.at[col],
                    (y, zz * 8 + g * pairs + turn),
                )

        @pl.when(mine // pairs == g)
        def _():
            fin[col] = outb[g, z, pl.ds(pl.multiple_of(lax.rem(mine, pairs) * piece, piece), piece), :]

        @pl.when(mine // pairs != g)
        def _():
            last_copy(g).start()

    for g in range(GROUPS):
        start_over_z(g)
    la_start()
    start_over_y(0)
    first_start(0)
    start_over_y(1)
    lb_start()
    first_near(0)
    start_over_y(2)
    start_over_y(3)
    first_far(0)
    first_start(1)
    lb_near()
    seconds_near(0)
    first_near(1)
    first_far(1)
    la_near()
    lb_far()
    first_start(2)
    seconds_far(0)
    seconds_near(1)
    cycle(0)
    first_near(2)
    first_far(2)
    la_far()
    ladder()
    first_start(3)
    cycle_middle(0)
    seconds_far(1)
    cycle(1)
    seconds_near(2)
    cycle_end(0)
    first_near(3)
    first_far(3)
    ladder_middle()
    cycle_middle(1)
    seconds_far(2)
    cycle(2)
    cycle_end(1)
    ladder_end()
    seconds_near(3)
    cycle_middle(2)
    seconds_far(3)
    cycle(3)
    cycle_end(2)
    cycle_middle(3)
    cycle_end(3)

    for step in range(1, 8 * N):
        source = lax.rem(col + step, 8 * N)
        arrived(fin.at[source], fin_sem.at[source])
    fin_ref[...] = fin[...]
    for copy in started:
        copy.wait_send()
    for g in range(GROUPS):

        @pl.when(y != 2 * (g % 2))
        def _():
            over_z(g).wait_send()

        @pl.when(z != 2 * (g % 2))
        def _():
            over_y(g, middle).wait_send()

        @pl.when(mine // pairs != g)
        def _():
            last_copy(g).wait_send()


def per_device(
    ladder_amps,
    ladder_integrals,
    cycle_amps,
    cycle_integrals,
    amp_screen,
    integral_screen,
    occupied_i,
    occupied_j,
    virtual_a,
    virtual_b,
):
    tile = virtual_b.shape[0]
    pair_count = occupied_j.shape[0]
    local_i = occupied_i.shape[0]
    local_a = virtual_a.shape[0]
    col = lax.axis_index("col")
    col_count = lax.axis_size("col")

    local_cols = ladder_amps.shape[1]
    mine = lax.dynamic_slice_in_dim(amp_screen, (col * local_cols) // (tile * tile), 1, axis=1)
    amp_mask = jnp.broadcast_to(mine[:, None, :], (local_i, pair_count, 1)).reshape(-1, 1)
    la = ladder_amps * amp_mask.astype(jnp.bfloat16)
    int_mask = jnp.repeat(jnp.repeat(integral_screen, tile, axis=0), tile, axis=1).astype(jnp.bfloat16)
    lb = ladder_integrals * int_mask

    all_i, local_k, _ = cycle_amps.shape
    s = cycle_amps.reshape(N, all_i // N, local_k, GROUPS, 8 // GROUPS, local_a, tile)
    s = s.transpose(3, 0, 4, 1, 5, 2, 6)
    s = s.reshape(all_i * 8 * local_a, local_k * tile)

    rows, depth = s.shape
    nc = cycle_integrals.shape[1]
    lm, lk = la.shape
    lrows, ln = lb.shape
    quarter = rows // GROUPS // N
    piece = rows // N // 8
    f32, bf16 = jnp.float32, jnp.bfloat16
    dma = pltpu.SemaphoreType.DMA
    vmem = pl.BlockSpec(memory_space=pltpu.VMEM)
    ladder, cycle = pl.pallas_call(
        kernel,
        out_shape=(
            jax.ShapeDtypeStruct((lm, ln), f32),
            jax.ShapeDtypeStruct((col_count, piece, nc), bf16),
        ),
        in_specs=[vmem] * 4,
        out_specs=(vmem, vmem),
        scratch_shapes=[
            pltpu.VMEM((rows, depth), bf16),
            pltpu.VMEM((N, N, 2, rows, depth), bf16),
            pltpu.VMEM((N, 2, lm, lk), bf16),
            pltpu.VMEM((N, lrows // N, N * ln), bf16),
            pltpu.VMEM((N, lm, ln), f32),
            pltpu.VMEM((2, lm // 2, ln), f32),
            pltpu.VMEM((2, lm, ln), f32),
            pltpu.VMEM((GROUPS, N, N, quarter, nc), f32),
            pltpu.VMEM((GROUPS, 2, N // 2, quarter, nc), f32),
            pltpu.VMEM((GROUPS, 2, N, quarter, nc), f32),
            pltpu.VMEM((GROUPS, N, quarter, nc), bf16),
            pltpu.VMEM((col_count, piece, nc), bf16),
            dma((SENDS,)),
            dma((GROUPS,)),
            dma((N, N, 2, GROUPS, 2)),
            dma((N, 2, 2)),
            dma((N,)),
            dma((N, 2)),
            dma((4,)),
            dma((GROUPS, 4)),
            dma((col_count,)),
            dma((2,)),
        ],
        compiler_params=pltpu.CompilerParams(
            collective_id=0, has_side_effects=True, vmem_limit_bytes=56 * 2**20
        ),
        cost_estimate=pl.CostEstimate(
            flops=2 * (N * rows * N * 2 * depth * nc + lm * N * 2 * lk * N * ln),
            bytes_accessed=8 * 2**20,
            transcendentals=0,
        ),
    )(s, la, lb, cycle_integrals)

    j_local = nc // tile
    cycle = cycle.reshape(col_count, local_i, local_a, j_local, tile).transpose(1, 0, 3, 2, 4)
    cycle = cycle.reshape(local_i * pair_count, local_a * tile)
    residual = ladder + cycle.astype(f32)
    virtual_sum = (virtual_a[:, None] + virtual_b[None, :]).reshape(-1)
    occupied_sum = (occupied_i[:, None] + occupied_j[None, :]).reshape(-1)
    denominator = virtual_sum[None, :] - occupied_sum[:, None]
    return residual / denominator


def solution(mesh):
    placed = (
        P("row", "col"),
        P("row", "col"),
        P(None, "col", "row"),
        P("row", "col"),
        P("row", None),
        P("row", "col"),
        P("row"),
        P(),
        P("col"),
        P(),
    )
    return jax.shard_map(
        per_device, mesh=mesh, in_specs=placed, out_specs=P("row", "col"), check_vma=False
    )
```

time: 195 us -> 171 us (0.88); the launches traced: 193 us -> 171 us
  Pallas kernels: 176 us -> 154 us
    pallas_call x1, Pallas kernels: 176 us -> 154 us  [per_device(): pl.pallas_call(kernel, out_shape=(jax.ShapeDtypeStruct((lm, ln), f32), ja...]
where the time goes in v2:
time: 171 us
  Pallas kernels  154 us (90%)
  local copies, waits for them, and re-layouts  13.4 us (8%)
  other arithmetic  3.41 us (2%)
    pallas_call x1, Pallas kernels, per_device(): pl.pallas_call(kernel, out_shape=(jax.ShapeDtypeStruct((lm, ln), f32), ja...  154 us
    convert_element_type x3, local copies, waits for them, and re-layouts, per_device(): residual = ladder + cycle.astype(f32)  5.88 us
    reshape x2, local copies, waits for them, and re-layouts, per_device(): cycle_amps.reshape(N, all_i // N, local_k, GROUPS, 8 // GROUPS, local_a,...  4.76 us

profile of v2, /device:TPU:7, one launch (start us, length us, event | category | flops | bytes accessed | tf_op | source)
XLA Modules:
  0.0 171.1 jit_solution(3033955809645677104)
XLA Ops:
  0.0 3.1 %reshape.64 = bf16[4,8,10,4,2,2,64]{6,5,4,3,1,0,2:T(2,128)(2,1)S(1)} reshape(bf16[32,10,1024]{2,0,1:T(8,128)(2,1)} %param.12) | data formatting | bytes 1310720 | tf_op jit(solution)/shard_map/reshape | solution.py:521
  3.2 1.6 copy.18
  4.8 0.0 copy-start.7
  4.8 0.0 copy-start
  4.8 0.0 copy-start.8
  4.8 1.9 %reshape.65.s_ref = bf16[512,640]{1,0:T(8,128)(2,1)} reshape(bf16[4,4,2,8,2,10,64]{6,5,4,3,2,1,0:T(8,128)(2,1)S(1)} %bitcast.12) | data formatting | bytes 1310720 | tf_op jit(solution)/shard_map/reshape | solution.py:523
  6.7 0.0 copy-start.2
  6.7 0.0 copy-done.7
  6.7 0.1 broadcast_in_dim.6
  6.8 0.1 convert_element_type.40
  6.9 0.0 copy-done
  6.9 1.2 broadcast_multiply_fusion.la_ref
  8.0 0.0 copy-done.8
  8.0 0.1 broadcast_in_dim.7
  8.1 0.1 convert_element_type.42
  8.2 0.1 broadcast_in_dim.8
  8.3 0.3 copy.15
  8.5 0.0 copy-done.2
  8.6 0.9 mul.17.lb_ref
  9.5 154.2 %shard_map.100 = (f32[1536,128]{1,0:T(8,128)}, bf16[32,16,384]{2,1,0:T(8,128)(2,1)}) custom-call(bf16[512,640]{1,0:T(8,128)(2,1)} %reshape.65.s_ref, bf16[1536,256]{1,0:T(8,128)(2,1)} %broadcast_multiply_fusion.la_ref, bf16[2048,128]{1,0:T(8,128)(2,1)} %mul.17.lb_ref, bf16[5120,384]{1,0:T(8,128)(2,1)} %cb_ref.1), custom_call_target="tpu_custom_call" | custom-call | flops 11274289152 | bytes 8388608 | tf_op jit(solution)/shard_map/pallas_call | solution.py:534
  163.7 1.5 reshape.67
  165.3 2.0 %copy.16 = f32[8,32,6,2,64]{4,3,2,1,0:T(2,128)} copy(f32[8,32,6,2,64]{4,2,3,0,1:T(8,128)S(1)} %bitcast.11) | data formatting | bytes 1572864 | tf_op jit(solution)/shard_map/convert_element_type | solution.py:579
  167.2 0.0 copy-start.3
  167.2 0.0 copy-start.4
  167.2 0.0 copy-start.5
  167.2 0.0 copy-start.6
  167.2 0.0 copy-start.1
  167.2 2.4 %reshape.66 = f32[1536,128]{1,0:T(8,128)S(1)} reshape(f32[8,32,6,2,64]{4,3,2,1,0:T(2,128)} %copy.16) | data formatting | bytes 1572864 | tf_op jit(solution)/shard_map/convert_element_type | solution.py:579
  169.7 0.0 copy-done.3
  169.7 0.0 copy-done.4
  169.7 0.1 broadcast_add_fusion
  169.7 0.1 add.56
  169.8 0.0 copy-done.5
  169.8 0.0 copy-done.6
  169.8 0.1 broadcast_add_fusion.1
  169.9 0.1 add.52
  170.0 0.0 copy-done.1
  170.0 1.2 subtract_divide_fusion
  (2 shorter events, 0.0 us)
Async XLA Ops:
  4.8 1.9 %copy-start.7 = (s32[8,2]{0,1:T(2,128)S(1)}, s32[8,2]{0,1:T(2,128)}, u32[]{:S(2)}) copy-start(s32[8,2]{0,1:T(2,128)} %param.14) | copy-start | bytes 196
  4.8 2.1 %copy-start = (bf16[1536,256]{1,0:T(8,128)(2,1)S(1)}, bf16[1536,256]{1,0:T(8,128)(2,1)}, u32[]{:S(2)}) copy-start(bf16[1536,256]{1,0:T(8,128)(2,1)} %param.10) | copy-start | bytes 2359300
  4.8 3.2 %copy-start.8 = (s32[32,2]{0,1:T(2,128)S(1)}, s32[32,2]{0,1:T(2,128)}, u32[]{:S(2)}) copy-start(s32[32,2]{0,1:T(2,128)} %param.15) | copy-start | bytes 772
  6.7 1.9 %copy-start.2 = (bf16[2048,128]{1,0:T(8,128)(2,1)S(1)}, bf16[2048,128]{1,0:T(8,128)(2,1)}, u32[]{:S(2)}) copy-start(bf16[2048,128]{1,0:T(8,128)(2,1)} %param.11) | copy-start | bytes 1572868
  167.2 2.4 %copy-start.3 = (f32[192]{0:T(256)S(1)}, f32[192]{0:T(256)}, u32[]{:S(2)}) copy-start(f32[192]{0:T(256)} %param.17) | copy-start | bytes 2308
  167.2 2.4 %copy-start.4 = (f32[8]{0:T(128)S(1)}, f32[8]{0:T(128)}, u32[]{:S(2)}) copy-start(f32[8]{0:T(128)} %param.16) | copy-start | bytes 100
  167.2 2.6 %copy-start.5 = (f32[64]{0:T(128)S(1)}, f32[64]{0:T(128)}, u32[]{:S(2)}) copy-start(f32[64]{0:T(128)} %param.19) | copy-start | bytes 772
  167.2 2.6 %copy-start.6 = (f32[2]{0:T(128)S(1)}, f32[2]{0:T(128)}, u32[]{:S(2)}) copy-start(f32[2]{0:T(128)} %param.18) | copy-start | bytes 28
  167.2 2.8 %copy-start.1 = (f32[1536,128]{1,0:T(8,128)S(1)}, f32[1536,128]{1,0:T(8,128)}, u32[]{:S(2)}) copy-start(f32[1536,128]{1,0:T(8,128)} %get-tuple-element.7) | copy-start | bytes 2359300

commit v3 on v2

--- a/solution.py
+++ b/solution.py
@@ -14,16 +14,24 @@
 
 
 def axis_order(core):
-    return (core, core, core, core)
+    return (1, 1, core, 0)
 
 
 def kernel(
+    tile_size,
+    amps_hbm,
+    la_hbm,
+    lb_hbm,
+    cb_hbm,
+    amp_screen,
+    integral_screen,
+    out_ref,
+    amps,
+    amps_wide,
     s_ref,
     la_ref,
     lb_ref,
     cb_ref,
-    lad_ref,
-    fin_ref,
     middle,
     a_buf,
     la_buf,
@@ -60,6 +68,13 @@
         return (yy, zz * 8 + xx * 2 + core)
 
     sibling = device(y, z, x, 1 - c)
+    copies = [
+        pltpu.make_async_copy(src, dst, local_sem.at[n])
+        for n, (src, dst) in enumerate(((amps_hbm, amps), (la_hbm, la_ref), (lb_hbm, lb_ref), (cb_hbm, cb_ref)))
+    ]
+    for copy in copies:
+        copy.start()
+
     rows, depth = s_ref.shape
     group = rows // GROUPS
     half = group // 2
@@ -73,6 +88,49 @@
         greet((y, lax.rem(col + step, 8 * N)))
     for step in range(1, N):
         greet((wrap(y + step), col))
+
+    blocks, local_k, lanes = amps.shape[0] // 8, amps.shape[1], 128
+    stride = amps_wide.shape[1] // amps.shape[0]
+    low = lax.broadcasted_iota(jnp.int32, (8, lanes), 1) < lanes // 2
+
+    def joined(left, right):
+        first_halves = jnp.where(low, left, pltpu.roll(right, lanes // 2, 1))
+        second_halves = jnp.where(low, pltpu.roll(left, lanes // 2, 1), right)
+        return first_halves, second_halves
+
+    copies[0].wait()
+    for i in range(amps.shape[0]):
+        for t in range(8):
+            wide = amps[i, :, t * lanes : (t + 1) * lanes].astype(jnp.float32)
+            amps_wide[t, pl.ds(i * stride, local_k), :] = wide
+
+    @pl.loop(0, blocks)
+    def _(ib):
+        for t in range(8):
+            pairs = 8 // GROUPS
+            row = (t // pairs) * group + ib * (group // blocks) + (t % pairs) * 16
+            for m in range(local_k // 2):
+                left, right = (
+                    amps_wide[t, pl.ds(ib * 8 * stride + k, 8, stride=stride), :]
+                    for k in (2 * m, 2 * m + 1)
+                )
+                s_ref[pl.ds(pl.multiple_of(row, 16), 16), m * lanes : (m + 1) * lanes] = jnp.concatenate(
+                    joined(left, right), axis=0
+                ).astype(s_ref.dtype)
+
+    copies[1].wait()
+    ladder_tile = (col * la_ref.shape[1]) // tile_size
+    pair_count = la_ref.shape[0] // amp_screen.shape[0]
+    for i in range(amp_screen.shape[0]):
+        part = pl.ds(i * pair_count, pair_count)
+        keep = amp_screen[i, ladder_tile].astype(jnp.float32).astype(la_ref.dtype)
+        la_buf[z, c, part, :] = la_ref[part, :] * keep
+    copies[2].wait()
+    side = lb_ref.shape[0] // integral_screen.shape[0]
+    for p in range(integral_screen.shape[0]):
+        part = pl.ds(p * side, side)
+        keep = jnp.where(low[:1], integral_screen[p, 0], integral_screen[p, 1])
+        lb_ref[part, :] = lb_ref[part, :] * keep.astype(jnp.float32).astype(lb_ref.dtype)
 
     pl.semaphore_wait(barrier, 8 * N + N - 2)
 
@@ -123,13 +181,13 @@
             ref, sem = slot(at, h)
             send(ref, ref, sem, other)
 
-    def ring_near(slot, at, plus, minus):
-        ref, sem = slot(wrap(at - 1), 0)
-        arrived(ref, sem)
-        send(ref, ref, sem, plus)
-        ref, sem = slot(wrap(at + 1), 1)
-        arrived(ref, sem)
-        send(ref, ref, sem, minus)
+    def ring_forward(slot, at, plus, minus):
+        for h, source, other in ((0, wrap(at - 1), plus), (1, wrap(at + 1), minus)):
+            ref, sem = slot(source, h)
+            arrived(ref, sem)
+            send(ref, ref, sem, other)
+
+    def ring_near(slot, at):
         arrived(*slot(wrap(at - 1), 1))
         arrived(*slot(wrap(at + 1), 0))
 
@@ -209,33 +267,35 @@
             over_y(g, middle).wait_recv()
 
     width = lb_ref.shape[1]
-    for step in range(1, N):
-        to = wrap(x + step)
-        send(
-            lb_ref.at[pl.ds(pl.multiple_of(to * lb_rows, lb_rows), lb_rows)],
-            lb_buf.at[y, :, pl.ds(pl.multiple_of(x * width, width), width)],
-            lx_sem.at[x],
-            device(y, z, to, c),
-        )
+    def lb_exchange():
+        for step in range(1, N):
+            to = wrap(x + step)
+            send(
+                lb_ref.at[pl.ds(pl.multiple_of(to * lb_rows, lb_rows), lb_rows)],
+                lb_buf.at[y, :, pl.ds(pl.multiple_of(x * width, width), width)],
+                lx_sem.at[x],
+                device(y, z, to, c),
+            )
+
     keep_lb = pltpu.make_async_copy(
         lb_ref.at[pl.ds(pl.multiple_of(x * lb_rows, lb_rows), lb_rows)],
         lb_buf.at[y, :, pl.ds(pl.multiple_of(x * width, width), width)],
-        local_sem.at[0],
+        local_sem.at[4],
     )
     keep_lb.start()
-    keep_la = pltpu.make_async_copy(la_ref, la_buf.at[z, c], local_sem.at[1])
-    keep_la.start()
 
     def la_own(p, h=None):
         return la_slot(p, c, h)
 
     def la_start():
-        keep_la.wait()
         ring_start(la_own, z, z_plus, z_minus)
         share(*la_slot(z, c))
 
+    def la_forward():
+        ring_forward(la_own, z, z_plus, z_minus)
+
     def la_near():
-        ring_near(la_own, z, z_plus, z_minus)
+        ring_near(la_own, z)
         for q in (wrap(z - 1), wrap(z + 1)):
             share(*la_slot(q, c))
 
@@ -250,10 +310,11 @@
             arrived(lb_buf.at[y, :, pl.ds(pl.multiple_of(source * width, width), width)], lx_sem.at[source])
         ring_start(lb_slot, y, y_plus, y_minus)
 
-    def lb_near():
-        ring_near(lb_slot, y, y_plus, y_minus)
-
-    def lb_far():
+    def lb_forward():
+        ring_forward(lb_slot, y, y_plus, y_minus)
+
+    def lb_end():
+        ring_near(lb_slot, y)
         ring_far(lb_slot, y)
 
     z_first = axis_order(c)
@@ -278,9 +339,13 @@
         ring_start(slot, *ring)
         share(*slot(ring[0]))
 
+    def second_forward(g, k):
+        slot, ring = second(g, k)
+        ring_forward(slot, *ring)
+
     def second_near(g, k):
         slot, ring = second(g, k)
-        ring_near(slot, *ring)
+        ring_near(slot, ring[0])
         for p in (wrap(ring[0] - 1), wrap(ring[0] + 1)):
             share(*slot(p))
 
@@ -295,9 +360,13 @@
         ring_start(slot, *ring)
         second_start(g, 0)
 
+    def first_forward(g):
+        slot, ring = first(g)
+        ring_forward(slot, *ring)
+
     def first_near(g):
         slot, ring = first(g)
-        ring_near(slot, *ring)
+        ring_near(slot, ring[0])
         second_start(g, 1)
         second_start(g, 2)
 
@@ -305,14 +374,6 @@
         slot, ring = first(g)
         ring_far(slot, ring[0])
         second_start(g, 3)
-
-    def seconds_near(g):
-        for k in range(N):
-            second_near(g, k)
-
-    def seconds_far(g):
-        for k in range(N):
-            second_far(g, k)
 
     tile = 256
     lk = la_ref.shape[1]
@@ -341,7 +402,7 @@
         reduce_middle(lc, lc_a, lc_b, lc_sem, x, x_plus, x_minus)
 
     def ladder_end():
-        lad_ref[...] = reduce_end(lc, lc_b, lc_sem, x)
+        out_ref[...] = reduce_end(lc, lc_b, lc_sem, x)
 
     def reduce_start(ref, land, sem, at, plus, minus):
         size = ref.shape[1] // 2
@@ -422,58 +483,115 @@
         def _():
             last_copy(g).start()
 
-    for g in range(GROUPS):
-        start_over_z(g)
+    start_over_z(2)
+    start_over_z(0)
+    start_over_z(1)
+    start_over_z(3)
+    lb_exchange()
+    start_over_y(2)
+    start_over_y(0)
+    first_start(2)
+    start_over_y(1)
+    first_start(1)
+    lb_start()
+    first_start(0)
+    first_forward(1)
     la_start()
-    start_over_y(0)
-    first_start(0)
-    start_over_y(1)
-    lb_start()
+    second_forward(0, 0)
+    first_forward(0)
+    first_near(1)
+    start_over_y(3)
+    second_forward(1, 1)
+    second_forward(1, 0)
+    la_forward()
+    first_forward(2)
+    first_far(1)
     first_near(0)
-    start_over_y(2)
-    start_over_y(3)
+    second_forward(1, 3)
+    second_far(0, 0)
     first_far(0)
-    first_start(1)
-    lb_near()
-    seconds_near(0)
-    first_near(1)
-    first_far(1)
+    lb_forward()
     la_near()
-    lb_far()
-    first_start(2)
-    seconds_far(0)
-    seconds_near(1)
+    first_near(2)
+    first_start(3)
+    second_far(1, 1)
+    la_far()
+    second_near(0, 0)
+    second_near(1, 1)
+    second_forward(0, 3)
+    second_forward(1, 2)
+    second_near(1, 0)
+    second_forward(2, 1)
+    second_near(1, 3)
+    second_near(1, 2)
+    second_far(1, 0)
+    second_forward(0, 2)
+    second_forward(0, 1)
+    second_far(1, 3)
+    second_near(0, 2)
+    first_forward(3)
+    lb_end()
+    first_near(3)
+    ladder()
+    second_far(1, 2)
+    second_forward(3, 1)
+    second_far(0, 3)
+    second_forward(3, 0)
+    second_near(0, 1)
+    second_far(2, 1)
+    second_forward(2, 2)
+    second_near(0, 3)
+    second_forward(3, 2)
+    second_near(3, 2)
+    second_near(3, 1)
+    first_far(2)
+    second_far(0, 2)
+    second_far(0, 1)
+    second_near(3, 0)
+    first_far(3)
+    copies[3].wait()
+    cycle(1)
+    second_near(2, 2)
     cycle(0)
-    first_near(2)
-    first_far(2)
-    la_far()
-    ladder()
-    first_start(3)
+    second_forward(3, 3)
+    second_far(3, 1)
+    second_far(3, 0)
+    second_near(3, 3)
+    second_forward(2, 0)
+    cycle_middle(1)
+    second_near(2, 1)
+    second_far(2, 2)
+    second_far(3, 2)
+    second_forward(2, 3)
+    second_far(3, 3)
+    second_near(2, 0)
+    second_near(2, 3)
     cycle_middle(0)
-    seconds_far(1)
-    cycle(1)
-    seconds_near(2)
+    second_far(2, 0)
+    ladder_middle()
+    second_far(2, 3)
+    cycle(3)
+    cycle(2)
+    cycle_middle(3)
+    cycle_middle(2)
     cycle_end(0)
-    first_near(3)
-    first_far(3)
-    ladder_middle()
-    cycle_middle(1)
-    seconds_far(2)
-    cycle(2)
     cycle_end(1)
+    cycle_end(3)
     ladder_end()
-    seconds_near(3)
-    cycle_middle(2)
-    seconds_far(3)
-    cycle(3)
     cycle_end(2)
-    cycle_middle(3)
-    cycle_end(3)
 
     for step in range(1, 8 * N):
         source = lax.rem(col + step, 8 * N)
         arrived(fin.at[source], fin_sem.at[source])
-    fin_ref[...] = fin[...]
+
+    @pl.loop(0, 8 * N)
+    def _(source):
+        for m in range(fin.shape[2] // lanes):
+            both = fin[source, :, m * lanes : (m + 1) * lanes].astype(jnp.float32)
+            for n, value in enumerate(joined(both[:8], both[8:])):
+                at = pl.ds(source * (fin.shape[2] // lanes * 2) + 2 * m + n, 8, stride=pair_count)
+                out_ref[at, :] = out_ref[at, :] + value
+
     for copy in started:
         copy.wait_send()
     for g in range(GROUPS):
@@ -504,42 +622,30 @@
     virtual_b,
 ):
     tile = virtual_b.shape[0]
-    pair_count = occupied_j.shape[0]
-    local_i = occupied_i.shape[0]
-    local_a = virtual_a.shape[0]
-    col = lax.axis_index("col")
     col_count = lax.axis_size("col")
-
-    local_cols = ladder_amps.shape[1]
-    mine = lax.dynamic_slice_in_dim(amp_screen, (col * local_cols) // (tile * tile), 1, axis=1)
-    amp_mask = jnp.broadcast_to(mine[:, None, :], (local_i, pair_count, 1)).reshape(-1, 1)
-    la = ladder_amps * amp_mask.astype(jnp.bfloat16)
-    int_mask = jnp.repeat(jnp.repeat(integral_screen, tile, axis=0), tile, axis=1).astype(jnp.bfloat16)
-    lb = ladder_integrals * int_mask
-
-    all_i, local_k, _ = cycle_amps.shape
-    s = cycle_amps.reshape(N, all_i // N, local_k, GROUPS, 8 // GROUPS, local_a, tile)
-    s = s.transpose(3, 0, 4, 1, 5, 2, 6)
-    s = s.reshape(all_i * 8 * local_a, local_k * tile)
-
-    rows, depth = s.shape
+    all_i, local_k, ac = cycle_amps.shape
+    rows, depth = all_i * ac // tile, local_k * tile
     nc = cycle_integrals.shape[1]
-    lm, lk = la.shape
-    lrows, ln = lb.shape
+    lm, lk = ladder_amps.shape
+    lrows, ln = ladder_integrals.shape
     quarter = rows // GROUPS // N
     piece = rows // N // 8
+    padded_k = -(-local_k // 8) * 8
     f32, bf16 = jnp.float32, jnp.bfloat16
     dma = pltpu.SemaphoreType.DMA
-    vmem = pl.BlockSpec(memory_space=pltpu.VMEM)
-    ladder, cycle = pl.pallas_call(
-        kernel,
-        out_shape=(
-            jax.ShapeDtypeStruct((lm, ln), f32),
-            jax.ShapeDtypeStruct((col_count, piece, nc), bf16),
-        ),
-        in_specs=[vmem] * 4,
-        out_specs=(vmem, vmem),
+    hbm, smem = pl.BlockSpec(memory_space=pl.ANY), pl.BlockSpec(memory_space=pltpu.SMEM)
+    residual = pl.pallas_call(
+        functools.partial(kernel, tile * tile),
+        out_shape=jax.ShapeDtypeStruct((lm, ln), f32),
+        in_specs=[hbm] * 4 + [smem] * 2,
+        out_specs=pl.BlockSpec(memory_space=pltpu.VMEM),
         scratch_shapes=[
+            pltpu.VMEM((all_i, local_k, ac), bf16),
+            pltpu.VMEM((8, all_i * padded_k, ac // 8), f32),
+            pltpu.VMEM((rows, depth), bf16),
+            pltpu.VMEM((lm, lk), bf16),
+            pltpu.VMEM((lrows, ln), bf16),
+            pltpu.VMEM(cycle_integrals.shape, bf16),
             pltpu.VMEM((rows, depth), bf16),
             pltpu.VMEM((N, N, 2, rows, depth), bf16),
             pltpu.VMEM((N, 2, lm, lk), bf16),
@@ -561,7 +667,7 @@
             dma((4,)),
             dma((GROUPS, 4)),
             dma((col_count,)),
-            dma((2,)),
+            dma((5,)),
         ],
         compiler_params=pltpu.CompilerParams(
             collective_id=0, has_side_effects=True, vmem_limit_bytes=56 * 2**20
@@ -571,12 +677,8 @@
             bytes_accessed=8 * 2**20,
             transcendentals=0,
         ),
-    )(s, la, lb, cycle_integrals)
-
-    j_local = nc // tile
-    cycle = cycle.reshape(col_count, local_i, local_a, j_local, tile).transpose(1, 0, 3, 2, 4)
-    cycle = cycle.reshape(local_i * pair_count, local_a * tile)
-    residual = ladder + cycle.astype(f32)
+    )(cycle_amps, ladder_amps, ladder_integrals, cycle_integrals, amp_screen, integral_screen)
+
     virtual_sum = (virtual_a[:, None] + virtual_b[None, :]).reshape(-1)
     occupied_sum = (occupied_i[:, None] + occupied_j[None, :]).reshape(-1)
     denominator = virtual_sum[None, :] - occupied_sum[:, None]

time: 171 us -> 136 us (0.80); the launches traced: 171 us -> 134 us
  Pallas kernels: 154 us -> 126 us
  local copies, waits for them, and re-layouts: 13.4 us -> 5.34 us
    pallas_call x1, Pallas kernels: 154 us -> 126 us  [per_device(): pl.pallas_call(functools.partial(kernel, tile * tile), out_shape=jax.Shap...]
    reshape x3 -> x0, local copies, waits for them, and re-layouts: 6.64 us -> none  [the longest x2 4.76 us: per_device(): cycle_amps.reshape(N, all_i // N, local_k, GROUPS, 8 // GROUPS, local_a,...]
    convert_element_type x6 -> x0, local copies, waits for them, and re-layouts: 6.34 us -> none  [the longest x3 5.88 us: per_device(): residual = ladder + cycle.astype(f32)]
    unnamed x18 -> x11, local copies, waits for them, and re-layouts: 0.04 us -> 5.18 us
    mul x2 -> x0, other arithmetic: 2.1 us -> none  [the longest x1 1.15 us: per_device(): la = ladder_amps * amp_mask.astype(jnp.bfloat16)]
where the time goes in v3:
time: 136 us; the launch traced here: 134 us
  Pallas kernels  126 us (93%)
  local copies, waits for them, and re-layouts  5.34 us (4%)
  other arithmetic  2.43 us (2%)
    pallas_call x1, Pallas kernels, per_device(): pl.pallas_call(functools.partial(kernel, tile * tile), out_shape=jax.Shap...  126 us
    unnamed x11, local copies, waits for them, and re-layouts  5.18 us

profile of v3, /device:TPU:7, one launch (start us, length us, event | category | flops | bytes accessed | tf_op | source)
XLA Modules:
  0.0 133.6 jit_solution(12676258537585928310)
XLA Ops:
  0.0 2.5 %copy.11.amps_hbm = bf16[32,10,1024]{2,1,0:T(8,128)(2,1)} copy(bf16[32,10,1024]{2,0,1:T(8,128)(2,1)} %param.12) | data formatting | bytes 1310720 | tf_op args[2]
  2.5 1.4 %copy.13.integral_screen = s32[32,2]{1,0:T(8,128)} copy(s32[32,2]{0,1:T(2,128)} %param.15) | data formatting | bytes 512 | tf_op args[5]
  3.8 1.3 %copy.12.amp_screen = s32[8,2]{1,0:T(8,128)} copy(s32[8,2]{0,1:T(2,128)} %param.14) | data formatting | bytes 128 | tf_op args[4]
  5.2 0.0 copy-start
  5.2 0.0 copy-start.1
  5.2 0.0 copy-start.2
  5.2 0.0 copy-start.3
  5.2 125.7 %shard_map.100 = f32[1536,128]{1,0:T(8,128)} custom-call(bf16[32,10,1024]{2,1,0:T(8,128)(2,1)} %copy.11.amps_hbm, bf16[1536,256]{1,0:T(8,128)(2,1)} %la_hbm.1, bf16[2048,128]{1,0:T(8,128)(2,1)} %lb_hbm.1, bf16[5120,384]{1,0:T(8,128)(2,1)} %cb_hbm.1, s32[8,2]{1,0:T(8,128)} %copy.12.amp_screen, s32[32,2]{1,0:T(8,128)} %copy.13.integral_screen), custom_call_target="tpu_custom_call" | custom-call | flops 11274289152 | bytes 8388608 | tf_op jit(solution)/shard_map/pallas_call | solution.py:637
  130.9 0.0 copy-done
  130.9 0.0 copy-done.1
  131.0 0.1 broadcast_add_fusion
  131.0 0.1 add.47
  131.1 0.0 copy-done.2
  131.1 0.0 copy-done.3
  131.1 0.1 broadcast_add_fusion.1
  131.2 0.1 add.43
  131.3 2.3 %subtract_divide_fusion = f32[1536,128]{1,0:T(8,128)} fusion(f32[1536,128]{1,0:T(8,128)} %shard_map.100, f32[1536]{0:T(1024)S(1)} %add.47, f32[128]{0:T(128)S(1)} %add.43), kind=kLoop, calls=%fused_computation | loop fusion | flops 393216 | bytes 1579520 | tf_op jit(solution)/shard_map/div | solution.py:685
Async XLA Ops:
  5.2 125.8 %copy-start = (f32[192]{0:T(256)S(1)}, f32[192]{0:T(256)}, u32[]{:S(2)}) copy-start(f32[192]{0:T(256)} %param.17) | copy-start | bytes 2308
  5.2 125.8 %copy-start.1 = (f32[8]{0:T(128)S(1)}, f32[8]{0:T(128)}, u32[]{:S(2)}) copy-start(f32[8]{0:T(128)} %param.16) | copy-start | bytes 100
  5.2 125.9 %copy-start.2 = (f32[64]{0:T(128)S(1)}, f32[64]{0:T(128)}, u32[]{:S(2)}) copy-start(f32[64]{0:T(128)} %param.19) | copy-start | bytes 772
  5.2 125.9 %copy-start.3 = (f32[2]{0:T(128)S(1)}, f32[2]{0:T(128)}, u32[]{:S(2)}) copy-start(f32[2]{0:T(128)} %param.18) | copy-start | bytes 28

commit v4 on v3

--- a/solution.py
+++ b/solution.py
@@ -9,7 +9,7 @@
 
 MESH = pl.DeviceIdType.MESH
 N = 4
-SENDS = 280
+SENDS = 296
 GROUPS = 4
 
 
@@ -25,9 +25,15 @@
     cb_hbm,
     amp_screen,
     integral_screen,
+    occupied_i,
+    occupied_j,
+    virtual_a,
+    virtual_b,
     out_ref,
     amps,
-    amps_wide,
+    screened,
+    gaps,
+    ladder_ji,
     s_ref,
     la_ref,
     lb_ref,
@@ -89,48 +95,63 @@
     for step in range(1, N):
         greet((wrap(y + step), col))
 
-    blocks, local_k, lanes = amps.shape[0] // 8, amps.shape[1], 128
-    stride = amps_wide.shape[1] // amps.shape[0]
-    low = lax.broadcasted_iota(jnp.int32, (8, lanes), 1) < lanes // 2
+    local_k, blocks, lanes = amps.shape[0], amps.shape[1] // 8, 128
+    low = lax.broadcasted_iota(jnp.int32, (1, lanes), 1) < lanes // 2
 
     def joined(left, right):
         first_halves = jnp.where(low, left, pltpu.roll(right, lanes // 2, 1))
         second_halves = jnp.where(low, pltpu.roll(left, lanes // 2, 1), right)
         return first_halves, second_halves
 
-    copies[0].wait()
-    for i in range(amps.shape[0]):
-        for t in range(8):
-            wide = amps[i, :, t * lanes : (t + 1) * lanes].astype(jnp.float32)
-            amps_wide[t, pl.ds(i * stride, local_k), :] = wide
-
-    @pl.loop(0, blocks)
-    def _(ib):
-        for t in range(8):
-            pairs = 8 // GROUPS
-            row = (t // pairs) * group + ib * (group // blocks) + (t % pairs) * 16
+    pairs = 8 // GROUPS
+
+    def permute(g):
+        for t in range(g * pairs, (g + 1) * pairs):
+            row = g * group + (t % pairs) * 16
             for m in range(local_k // 2):
                 left, right = (
-                    amps_wide[t, pl.ds(ib * 8 * stride + k, 8, stride=stride), :]
-                    for k in (2 * m, 2 * m + 1)
+                    amps[k, :, t * lanes : (t + 1) * lanes].astype(jnp.float32) for k in (2 * m, 2 * m + 1)
                 )
-                s_ref[pl.ds(pl.multiple_of(row, 16), 16), m * lanes : (m + 1) * lanes] = jnp.concatenate(
-                    joined(left, right), axis=0
-                ).astype(s_ref.dtype)
-
-    copies[1].wait()
+                both = joined(left, right)
+                for ib in range(blocks):
+                    s_ref[pl.ds(row + ib * (group // blocks), 16), m * lanes : (m + 1) * lanes] = jnp.concatenate(
+                        [value[ib * 8 : (ib + 1) * 8] for value in both], axis=0
+                    ).astype(s_ref.dtype)
+
+    copies[0].wait()
+    permute(0)
+
+    pair_count = la_ref.shape[0] // amp_screen.shape[1]
     ladder_tile = (col * la_ref.shape[1]) // tile_size
-    pair_count = la_ref.shape[0] // amp_screen.shape[0]
-    for i in range(amp_screen.shape[0]):
-        part = pl.ds(i * pair_count, pair_count)
-        keep = amp_screen[i, ladder_tile].astype(jnp.float32).astype(la_ref.dtype)
-        la_buf[z, c, part, :] = la_ref[part, :] * keep
-    copies[2].wait()
-    side = lb_ref.shape[0] // integral_screen.shape[0]
-    for p in range(integral_screen.shape[0]):
-        part = pl.ds(p * side, side)
-        keep = jnp.where(low[:1], integral_screen[p, 0], integral_screen[p, 1])
-        lb_ref[part, :] = lb_ref[part, :] * keep.astype(jnp.float32).astype(lb_ref.dtype)
+
+    def screen_amps():
+        copies[1].wait()
+        for i in range(amp_screen.shape[1]):
+            part = pl.ds(i * pair_count, pair_count)
+            keep = amp_screen[ladder_tile, i].astype(jnp.float32).astype(la_ref.dtype)
+            la_buf[z, c, part, :] = la_ref[part, :] * keep
+
+    def screen_integrals():
+        copies[2].wait()
+        side = lb_ref.shape[0] // integral_screen.shape[1]
+        for p in range(integral_screen.shape[1]):
+            part = pl.ds(p * side, side)
+            keep = jnp.where(low, integral_screen[0, p], integral_screen[1, p])
+            screened[part, :] = lb_ref[part, :] * keep.astype(jnp.float32).astype(lb_ref.dtype)
+
+    def energies():
+        lane = lax.broadcasted_iota(jnp.int32, (8, lanes), 1)
+        row = lax.broadcasted_iota(jnp.int32, (8, lanes), 0)
+        side = virtual_b.shape[0]
+        virtual = jnp.zeros((8, lanes), jnp.float32)
+        for b in range(side):
+            virtual = jnp.where(lax.rem(lane, side) == b, virtual_b[b], virtual)
+        virtual = virtual + jnp.where(low, virtual_a[0], virtual_a[1])
+        occupied = jnp.zeros((8, lanes), jnp.float32)
+        for i in range(occupied_i.shape[0]):
+            occupied = jnp.where(row == i, occupied_i[i], occupied)
+        for j in range(occupied_j.shape[0]):
+            gaps[j] = virtual - (occupied + occupied_j[j])
 
     pl.semaphore_wait(barrier, 8 * N + N - 2)
 
@@ -209,85 +230,90 @@
     def group_rows(g):
         return pl.ds(g * group, group)
 
-    def over_z(g):
-        part = group_rows(g)
+    def over_z(g, h):
+        part = pl.ds(g * group + h * half, half)
         return pltpu.make_async_remote_copy(
             src_ref=s_ref.at[part],
             dst_ref=middle.at[part],
-            send_sem=send_sem.at[SENDS - 1 - g],
-            recv_sem=middle_sem.at[g],
+            send_sem=send_sem.at[SENDS - 1 - 2 * g - h],
+            recv_sem=middle_sem.at[g, h],
             device_id=device(y, swapped(g), x, c),
             device_id_type=MESH,
         )
 
-    def over_y(g, ref):
-        part = group_rows(g)
+    def over_y(g, h, ref):
+        part = pl.ds(g * group + h * half, half)
         return pltpu.make_async_remote_copy(
             src_ref=ref.at[part],
             dst_ref=a_buf.at[z, x, c, part],
-            send_sem=send_sem.at[SENDS - 1 - GROUPS - g],
-            recv_sem=a_sem.at[z, x, c, g, 0],
+            send_sem=send_sem.at[SENDS - 1 - 2 * GROUPS - 2 * g - h],
+            recv_sem=a_sem.at[z, x, c, g, h],
             device_id=(swapped(g), col),
             device_id_type=MESH,
         )
 
     def start_over_z(g):
+        if g > 0:
+            permute(g)
+
         @pl.when(y != 2 * (g % 2))
         def _():
-            over_z(g).start()
+            for h in range(2):
+                over_z(g, h).start()
 
     def start_over_y(g):
         still = 2 * (g % 2)
 
-        @pl.when(y != still)
-        def _():
-            over_z(g).wait_recv()
-
+        def onward(h, ref):
             @pl.when(z != still)
             def _():
-                over_y(g, middle).start()
+                over_y(g, h, ref).start()
 
             @pl.when(z == still)
             def _():
-                a_buf[z, x, c, group_rows(g), :] = middle[group_rows(g), :]
+                part = pl.ds(g * group + h * half, half)
+                a_buf[z, x, c, part, :] = ref[part, :]
+
+        @pl.when(y != still)
+        def _():
+            for h in range(2):
+                over_z(g, h).wait_recv()
+                onward(h, middle)
 
         @pl.when(y == still)
         def _():
-            @pl.when(z != still)
-            def _():
-                over_y(g, s_ref).start()
-
-            @pl.when(z == still)
-            def _():
-                a_buf[z, x, c, group_rows(g), :] = s_ref[group_rows(g), :]
-
-    def end_over_y(g):
+            for h in range(2):
+                onward(h, s_ref)
+
+    def end_over_y(g, h):
         @pl.when(z != 2 * (g % 2))
         def _():
-            over_y(g, middle).wait_recv()
+            over_y(g, h, middle).wait_recv()
 
     width = lb_ref.shape[1]
     def lb_exchange():
+        screen_integrals()
+        keep_lb.start()
         for step in range(1, N):
             to = wrap(x + step)
             send(
-                lb_ref.at[pl.ds(pl.multiple_of(to * lb_rows, lb_rows), lb_rows)],
+                screened.at[pl.ds(pl.multiple_of(to * lb_rows, lb_rows), lb_rows)],
                 lb_buf.at[y, :, pl.ds(pl.multiple_of(x * width, width), width)],
                 lx_sem.at[x],
                 device(y, z, to, c),
             )
 
     keep_lb = pltpu.make_async_copy(
-        lb_ref.at[pl.ds(pl.multiple_of(x * lb_rows, lb_rows), lb_rows)],
+        screened.at[pl.ds(pl.multiple_of(x * lb_rows, lb_rows), lb_rows)],
         lb_buf.at[y, :, pl.ds(pl.multiple_of(x * width, width), width)],
         local_sem.at[4],
     )
-    keep_lb.start()
 
     def la_own(p, h=None):
         return la_slot(p, c, h)
 
     def la_start():
+        screen_amps()
         ring_start(la_own, z, z_plus, z_minus)
         share(*la_slot(z, c))
 
@@ -355,10 +381,15 @@
         share(*slot(wrap(ring[0] + 2)))
 
     def first_start(g):
-        end_over_y(g)
-        slot, ring = first(g)
-        ring_start(slot, *ring)
-        second_start(g, 0)
+        near = first(g), second(g, 0)
+        for h in range(2):
+            end_over_y(g, h)
+            for slot, (at, plus, minus) in near:
+                ref, sem = slot(at, h)
+                for other in (plus, minus) if h == 0 else (minus, plus):
+                    send(ref, ref, sem, other)
+        slot, ring = near[1]
+        share(*slot(ring[0]))
 
     def first_forward(g):
         slot, ring = first(g)
@@ -403,6 +434,8 @@
 
     def ladder_end():
         out_ref[...] = reduce_end(lc, lc_b, lc_sem, x)
+        for j in range(pair_count):
+            ladder_ji[j] = out_ref[pl.ds(j, 8, stride=pair_count), :]
 
     def reduce_start(ref, land, sem, at, plus, minus):
         size = ref.shape[1] // 2
@@ -423,7 +456,6 @@
         return ref[at] + land_b[0] + land_b[1]
 
     quarter = group // N
-    pairs = 8 // GROUPS
     piece = quarter // pairs
     mine = x * 2 + c
 
@@ -454,7 +486,7 @@
         return pltpu.make_async_remote_copy(
             src_ref=outb.at[g, z, pl.ds(pl.multiple_of(turn * piece, piece), piece)],
             dst_ref=fin.at[col],
-            send_sem=send_sem.at[SENDS - 1 - 2 * GROUPS - g],
+            send_sem=send_sem.at[SENDS - 1 - 4 * GROUPS - g],
             recv_sem=fin_sem.at[col],
             device_id=(y, z * 8 + g * pairs + turn),
             device_id_type=MESH,
@@ -483,114 +515,115 @@
         def _():
             last_copy(g).start()
 
+    start_over_z(1)
     start_over_z(2)
-    start_over_z(0)
-    start_over_z(1)
     start_over_z(3)
     lb_exchange()
+    start_over_y(1)
+    start_over_z(0)
     start_over_y(2)
+    first_start(1)
+    energies()
     start_over_y(0)
     first_start(2)
-    start_over_y(1)
-    first_start(1)
+    first_start(0)
     lb_start()
-    first_start(0)
-    first_forward(1)
+    first_forward(2)
+    second_forward(1, 0)
+    first_near(2)
+    start_over_y(3)
+    first_far(2)
+    first_forward(0)
+    first_near(0)
     la_start()
-    second_forward(0, 0)
-    first_forward(0)
-    first_near(1)
-    start_over_y(3)
-    second_forward(1, 1)
-    second_forward(1, 0)
-    la_forward()
-    first_forward(2)
-    first_far(1)
-    first_near(0)
-    second_forward(1, 3)
-    second_far(0, 0)
-    first_far(0)
     lb_forward()
-    la_near()
-    first_near(2)
-    first_start(3)
-    second_far(1, 1)
-    la_far()
-    second_near(0, 0)
-    second_near(1, 1)
-    second_forward(0, 3)
-    second_forward(1, 2)
-    second_near(1, 0)
-    second_forward(2, 1)
-    second_near(1, 3)
-    second_near(1, 2)
     second_far(1, 0)
     second_forward(0, 2)
     second_forward(0, 1)
+    first_forward(1)
+    second_forward(2, 3)
+    first_far(0)
+    second_forward(0, 0)
+    la_forward()
+    second_forward(0, 3)
+    second_near(0, 0)
+    lb_end()
+    second_forward(2, 2)
+    second_near(0, 1)
+    first_start(3)
+    second_far(2, 3)
+    first_near(1)
+    second_near(0, 3)
+    second_forward(2, 1)
+    second_far(0, 1)
+    second_near(2, 2)
+    second_far(0, 2)
+    second_far(0, 3)
+    second_far(0, 0)
+    second_near(2, 3)
+    second_near(0, 2)
+    second_near(1, 0)
+    first_far(1)
+    first_forward(3)
+    la_near()
+    second_forward(2, 0)
+    copies[3].wait()
+    cycle(0)
+    second_forward(1, 1)
+    second_near(2, 0)
+    la_far()
+    second_near(1, 1)
+    second_forward(3, 0)
+    second_far(2, 2)
+    second_near(3, 0)
+    second_forward(1, 2)
+    second_near(2, 1)
+    cycle_middle(0)
+    first_near(3)
+    second_near(1, 2)
+    second_forward(1, 3)
+    first_far(3)
+    second_far(2, 1)
+    second_near(1, 3)
+    second_far(2, 0)
+    ladder()
+    cycle(2)
+    second_far(1, 1)
+    second_far(1, 2)
+    second_forward(3, 2)
+    second_forward(3, 1)
     second_far(1, 3)
-    second_near(0, 2)
-    first_forward(3)
-    lb_end()
-    first_near(3)
-    ladder()
-    second_far(1, 2)
-    second_forward(3, 1)
-    second_far(0, 3)
-    second_forward(3, 0)
-    second_near(0, 1)
-    second_far(2, 1)
-    second_forward(2, 2)
-    second_near(0, 3)
-    second_forward(3, 2)
+    second_forward(3, 3)
+    second_far(3, 0)
+    second_near(3, 1)
     second_near(3, 2)
-    second_near(3, 1)
-    first_far(2)
-    second_far(0, 2)
-    second_far(0, 1)
-    second_near(3, 0)
-    first_far(3)
-    copies[3].wait()
+    second_near(3, 3)
+    cycle_middle(2)
+    ladder_middle()
+    second_far(3, 1)
+    second_far(3, 2)
+    second_far(3, 3)
     cycle(1)
-    second_near(2, 2)
-    cycle(0)
-    second_forward(3, 3)
-    second_far(3, 1)
-    second_far(3, 0)
-    second_near(3, 3)
-    second_forward(2, 0)
+    cycle(3)
     cycle_middle(1)
-    second_near(2, 1)
-    second_far(2, 2)
-    second_far(3, 2)
-    second_forward(2, 3)
-    second_far(3, 3)
-    second_near(2, 0)
-    second_near(2, 3)
-    cycle_middle(0)
-    second_far(2, 0)
-    ladder_middle()
-    second_far(2, 3)
-    cycle(3)
-    cycle(2)
+    cycle_end(0)
+    cycle_end(2)
     cycle_middle(3)
-    cycle_middle(2)
-    cycle_end(0)
     cycle_end(1)
+    ladder_end()
     cycle_end(3)
-    ladder_end()
-    cycle_end(2)
 
     for step in range(1, 8 * N):
         source = lax.rem(col + step, 8 * N)
         arrived(fin.at[source], fin_sem.at[source])
 
-    @pl.loop(0, 8 * N)
+    @pl.loop(0, 8 * N, unroll=4)
     def _(source):
         for m in range(fin.shape[2] // lanes):
             both = fin[source, :, m * lanes : (m + 1) * lanes].astype(jnp.float32)
             for n, value in enumerate(joined(both[:8], both[8:])):
-                at = pl.ds(source * (fin.shape[2] // lanes * 2) + 2 * m + n, 8, stride=pair_count)
-                out_ref[at, :] = out_ref[at, :] + value
+                j = source * (fin.shape[2] // lanes * 2) + 2 * m + n
+                out_ref[pl.ds(j, 8, stride=pair_count), :] = (ladder_ji[j] + value) / gaps[j]
 
     for copy in started:
         copy.wait_send()
@@ -598,11 +631,13 @@
 
         @pl.when(y != 2 * (g % 2))
         def _():
-            over_z(g).wait_send()
+            for h in range(2):
+                over_z(g, h).wait_send()
 
         @pl.when(z != 2 * (g % 2))
         def _():
-            over_y(g, middle).wait_send()
+            for h in range(2):
+                over_y(g, h, middle).wait_send()
 
         @pl.when(mine // pairs != g)
         def _():
@@ -630,18 +665,19 @@
     lrows, ln = ladder_integrals.shape
     quarter = rows // GROUPS // N
     piece = rows // N // 8
-    padded_k = -(-local_k // 8) * 8
     f32, bf16 = jnp.float32, jnp.bfloat16
     dma = pltpu.SemaphoreType.DMA
     hbm, smem = pl.BlockSpec(memory_space=pl.ANY), pl.BlockSpec(memory_space=pltpu.SMEM)
-    residual = pl.pallas_call(
+    return pl.pallas_call(
         functools.partial(kernel, tile * tile),
         out_shape=jax.ShapeDtypeStruct((lm, ln), f32),
-        in_specs=[hbm] * 4 + [smem] * 2,
+        in_specs=[hbm] * 4 + [smem] * 6,
         out_specs=pl.BlockSpec(memory_space=pltpu.VMEM),
         scratch_shapes=[
-            pltpu.VMEM((all_i, local_k, ac), bf16),
-            pltpu.VMEM((8, all_i * padded_k, ac // 8), f32),
+            pltpu.VMEM((local_k, all_i, ac), bf16),
+            pltpu.VMEM((lrows, ln), bf16),
+            pltpu.VMEM((occupied_j.shape[0], occupied_i.shape[0], ln), f32),
+            pltpu.VMEM((occupied_j.shape[0], occupied_i.shape[0], ln), f32),
             pltpu.VMEM((rows, depth), bf16),
             pltpu.VMEM((lm, lk), bf16),
             pltpu.VMEM((lrows, ln), bf16),
@@ -659,7 +695,7 @@
             pltpu.VMEM((GROUPS, N, quarter, nc), bf16),
             pltpu.VMEM((col_count, piece, nc), bf16),
             dma((SENDS,)),
-            dma((GROUPS,)),
+            dma((GROUPS, 2)),
             dma((N, N, 2, GROUPS, 2)),
             dma((N, 2, 2)),
             dma((N,)),
@@ -677,12 +713,18 @@
             bytes_accessed=8 * 2**20,
             transcendentals=0,
         ),
-    )(cycle_amps, ladder_amps, ladder_integrals, cycle_integrals, amp_screen, integral_screen)
-
-    virtual_sum = (virtual_a[:, None] + virtual_b[None, :]).reshape(-1)
-    occupied_sum = (occupied_i[:, None] + occupied_j[None, :]).reshape(-1)
-    denominator = virtual_sum[None, :] - occupied_sum[:, None]
-    return residual / denominator
+    )(
+        cycle_amps.transpose(1, 0, 2),
+        ladder_amps,
+        ladder_integrals,
+        cycle_integrals,
+        amp_screen.T,
+        integral_screen.T,
+        occupied_i,
+        occupied_j,
+        virtual_a,
+        virtual_b,
+    )
 
 
 def solution(mesh):

time: 136 us -> 126 us (0.926); the launches traced: 134 us -> 126 us
  local copies, waits for them, and re-layouts: 5.34 us -> 2.06 us
  other arithmetic: 2.43 us -> 0 us
  Pallas kernels: 126 us -> 124 us
    unnamed x11 -> x1, local copies, waits for them, and re-layouts: 5.18 us -> 2.06 us
    div x1 -> x0, other arithmetic: 2.29 us -> none  [per_device(): return residual / denominator]
    pallas_call x1, Pallas kernels: 126 us -> 124 us  [per_device(): pl.pallas_call(functools.partial(kernel, tile * tile), out_shape=jax.Shap...]
where the time goes in v4:
time: 126 us
  Pallas kernels  124 us (98%)
  local copies, waits for them, and re-layouts  2.06 us (2%)
    pallas_call x1, Pallas kernels, per_device(): pl.pallas_call(functools.partial(kernel, tile * tile), out_shape=jax.Shap...  124 us

profile of v4, /device:TPU:7, one launch (start us, length us, event | category | flops | bytes accessed | tf_op | source)
XLA Modules:
  0.0 126.3 jit_solution(10380655497322903670)
XLA Ops:
  0.0 124.2 %shard_map.100 = f32[1536,128]{1,0:T(8,128)} custom-call(bf16[10,32,1024]{2,1,0:T(8,128)(2,1)} %bitcast.3, bf16[1536,256]{1,0:T(8,128)(2,1)} %la_hbm.1, bf16[2048,128]{1,0:T(8,128)(2,1)} %lb_hbm.1, bf16[5120,384]{1,0:T(8,128)(2,1)} %cb_hbm.1, s32[2,8]{1,0:T(2,128)} %bitcast.4, s32[2,32]{1,0:T(2,128)} %bitcast.5, f32[8]{0:T(128)} %occupied_i.1, ...), custom_call_target="tpu_custom_call" | custom-call | flops 11274289152 | bytes 8388608 | tf_op jit(solution)/shard_map/pallas_call | solution.py:671
  124.3 2.1 %copy.12 = f32[1536,128]{1,0:T(8,128)} copy(f32[1536,128]{1,0:T(8,128)} %shard_map.100) | data formatting | bytes 1572864

commit v5 on v4

--- a/solution.py
+++ b/solution.py
@@ -9,12 +9,13 @@
 
 MESH = pl.DeviceIdType.MESH
 N = 4
-SENDS = 296
+SENDS = 304
 GROUPS = 4
+LAST = GROUPS - 1
 
 
 def axis_order(core):
-    return (1, 1, core, 0)
+    return (core, 1, 0, 1)
 
 
 def kernel(
@@ -48,6 +49,9 @@
     cc,
     cc_a,
     cc_b,
+    block_c,
+    block_a,
+    block_b,
     outb,
     fin,
     send_sem,
@@ -58,6 +62,7 @@
     lb_sem,
     lc_sem,
     cc_sem,
+    block_sem,
     fin_sem,
     local_sem,
 ):
@@ -357,7 +362,7 @@
 
     def second(g, k):
         f = z_first[g]
-        p = wrap(f * z + (1 - f) * x + (0, 3, 1, 2)[k])
+        p = wrap(f * z + (1 - f) * x + (0, 3, 1, 2)[k]) if g < LAST else swapped(g, k)
         return (lambda q, h=None: a_slot(f * p + (1 - f) * q, f * q + (1 - f) * p, g, h)), ring_of(1 - f)
 
     def second_start(g, k):
@@ -381,15 +386,16 @@
         share(*slot(wrap(ring[0] + 2)))
 
     def first_start(g):
-        near = first(g), second(g, 0)
+        near = (first(g), second(g, 0)) if g < LAST else (first(g),)
         for h in range(2):
             end_over_y(g, h)
             for slot, (at, plus, minus) in near:
                 ref, sem = slot(at, h)
                 for other in (plus, minus) if h == 0 else (minus, plus):
                     send(ref, ref, sem, other)
-        slot, ring = near[1]
-        share(*slot(ring[0]))
+        if g < LAST:
+            slot, ring = near[1]
+            share(*slot(ring[0]))
 
     def first_forward(g):
         slot, ring = first(g)
@@ -398,13 +404,15 @@
     def first_near(g):
         slot, ring = first(g)
         ring_near(slot, ring[0])
-        second_start(g, 1)
-        second_start(g, 2)
+        if g < LAST:
+            second_start(g, 1)
+            second_start(g, 2)
 
     def first_far(g):
         slot, ring = first(g)
         ring_far(slot, ring[0])
-        second_start(g, 3)
+        if g < LAST:
+            second_start(g, 3)
 
     tile = 256
     lk = la_ref.shape[1]
@@ -515,103 +523,160 @@
         def _():
             last_copy(g).start()
 
+    def block(k):
+        zz = swapped(LAST, k)
+        for xx in range(N):
+            arrived(a_buf.at[zz, xx, 1 - c, group_rows(LAST)], a_sem.at[zz, xx, 1 - c, LAST, 0])
+        total = jnp.zeros((group, cb_ref.shape[1]), jnp.float32)
+        for xx in range(N):
+            for core in range(2):
+                total += jnp.dot(
+                    a_buf[zz, xx, core, group_rows(LAST), :],
+                    cb_ref[pl.ds((xx * 2 + core) * depth, depth), :],
+                    preferred_element_type=jnp.float32,
+                )
+        for n in range(N):
+            block_c[k, n] = total[n * quarter : (n + 1) * quarter]
+        reduce_start(block_c.at[k], block_a.at[k], block_sem.at[k], y, y_plus, y_minus)
+
+    def block_middle(k):
+        reduce_middle(block_c.at[k], block_a.at[k], block_b.at[k], block_sem.at[k], y, y_plus, y_minus)
+
+    def block_copy(k, n):
+        other = k * 8 + LAST * pairs + n
+        copy = pltpu.make_async_remote_copy(
+            src_ref=outb.at[LAST, k, pl.ds(n * piece, piece)],
+            dst_ref=fin.at[col],
+            send_sem=send_sem.at[SENDS - 1 - 5 * GROUPS - pairs * k - n],
+            recv_sem=fin_sem.at[col],
+            device_id=(y, other),
+            device_id_type=MESH,
+        )
+        return other, copy
+
+    def block_end(k):
+        outb[LAST, k] = reduce_end(block_c.at[k], block_b.at[k], block_sem.at[k], y).astype(outb.dtype)
+        for n in range(pairs):
+            other, copy = block_copy(k, n)
+
+            @pl.when(col == other)
+            def _():
+                fin[col] = outb[LAST, k, pl.ds(n * piece, piece), :]
+
+            @pl.when(col != other)
+            def _():
+                copy.start()
+
+    start_over_z(0)
+    lb_exchange()
     start_over_z(1)
     start_over_z(2)
+    start_over_y(0)
     start_over_z(3)
-    lb_exchange()
     start_over_y(1)
-    start_over_z(0)
+    first_start(0)
+    energies()
+    first_start(1)
+    start_over_y(3)
+    first_forward(0)
+    second_forward(1, 0)
+    first_start(3)
+    first_forward(1)
+    first_near(1)
     start_over_y(2)
-    first_start(1)
-    energies()
-    start_over_y(0)
+    first_forward(3)
+    la_start()
+    second_near(1, 0)
+    second_forward(1, 1)
+    first_far(1)
+    second_forward(1, 3)
+    second_near(1, 1)
+    lb_start()
+    first_near(3)
+    second_forward(1, 2)
+    second_near(1, 3)
+    second_far(1, 0)
+    first_far(3)
+    second_start(3, 1)
+    second_start(3, 0)
+    second_far(1, 1)
+    second_far(1, 3)
+    first_near(0)
+    second_far(1, 2)
+    second_near(1, 2)
+    second_forward(3, 1)
+    la_forward()
+    lb_forward()
+    copies[3].wait()
+    cycle(1)
+    second_forward(3, 0)
+    second_forward(0, 2)
+    first_far(0)
     first_start(2)
-    first_start(0)
-    lb_start()
+    second_start(3, 3)
+    second_near(0, 2)
+    second_near(3, 1)
+    lb_end()
+    second_far(3, 0)
+    second_far(3, 1)
+    la_near()
+    cycle_middle(1)
+    second_near(3, 0)
+    second_forward(0, 0)
+    block(1)
+    second_near(0, 0)
+    second_forward(0, 1)
+    second_near(0, 1)
+    la_far()
     first_forward(2)
-    second_forward(1, 0)
+    block(0)
+    second_forward(0, 3)
     first_near(2)
-    start_over_y(3)
+    second_forward(3, 3)
+    second_start(3, 2)
+    second_near(3, 3)
+    ladder()
+    second_far(0, 2)
+    second_far(0, 1)
+    second_far(0, 0)
+    second_near(0, 3)
+    block_middle(0)
+    second_far(0, 3)
+    second_forward(2, 0)
+    second_forward(3, 2)
+    block_middle(1)
+    second_far(3, 3)
     first_far(2)
-    first_forward(0)
-    first_near(0)
-    la_start()
-    lb_forward()
-    second_far(1, 0)
-    second_forward(0, 2)
-    second_forward(0, 1)
-    first_forward(1)
+    cycle(0)
+    second_forward(2, 2)
+    block(3)
+    second_near(3, 2)
+    second_forward(2, 1)
     second_forward(2, 3)
-    first_far(0)
-    second_forward(0, 0)
-    la_forward()
-    second_forward(0, 3)
-    second_near(0, 0)
-    lb_end()
-    second_forward(2, 2)
-    second_near(0, 1)
-    first_start(3)
+    second_near(2, 1)
+    second_near(2, 3)
+    second_near(2, 0)
+    ladder_middle()
+    second_far(2, 0)
+    second_near(2, 2)
+    second_far(2, 2)
+    cycle_middle(0)
+    second_far(3, 2)
+    second_far(2, 1)
+    block_middle(3)
     second_far(2, 3)
-    first_near(1)
-    second_near(0, 3)
-    second_forward(2, 1)
-    second_far(0, 1)
-    second_near(2, 2)
-    second_far(0, 2)
-    second_far(0, 3)
-    second_far(0, 0)
-    second_near(2, 3)
-    second_near(0, 2)
-    second_near(1, 0)
-    first_far(1)
-    first_forward(3)
-    la_near()
-    second_forward(2, 0)
-    copies[3].wait()
-    cycle(0)
-    second_forward(1, 1)
-    second_near(2, 0)
-    la_far()
-    second_near(1, 1)
-    second_forward(3, 0)
-    second_far(2, 2)
-    second_near(3, 0)
-    second_forward(1, 2)
-    second_near(2, 1)
-    cycle_middle(0)
-    first_near(3)
-    second_near(1, 2)
-    second_forward(1, 3)
-    first_far(3)
-    second_far(2, 1)
-    second_near(1, 3)
-    second_far(2, 0)
-    ladder()
     cycle(2)
-    second_far(1, 1)
-    second_far(1, 2)
-    second_forward(3, 2)
-    second_forward(3, 1)
-    second_far(1, 3)
-    second_forward(3, 3)
-    second_far(3, 0)
-    second_near(3, 1)
-    second_near(3, 2)
-    second_near(3, 3)
+    block(2)
+    block_end(3)
     cycle_middle(2)
-    ladder_middle()
-    second_far(3, 1)
-    second_far(3, 2)
-    second_far(3, 3)
-    cycle(1)
-    cycle(3)
-    cycle_middle(1)
+    block_end(1)
+    block_end(0)
+    block_middle(2)
+    cycle_end(1)
     cycle_end(0)
     cycle_end(2)
-    cycle_middle(3)
-    cycle_end(1)
+    block_end(2)
     ladder_end()
-    cycle_end(3)
 
     for step in range(1, 8 * N):
         source = lax.rem(col + step, 8 * N)
@@ -639,9 +704,19 @@
             for h in range(2):
                 over_y(g, h, middle).wait_send()
 
-        @pl.when(mine // pairs != g)
-        def _():
-            last_copy(g).wait_send()
+        if g < LAST:
+
+            @pl.when(mine // pairs != g)
+            def _():
+                last_copy(g).wait_send()
+
+    for k in range(N):
+        for n in range(pairs):
+            other, copy = block_copy(k, n)
+
+            @pl.when(col != other)
+            def _():
+                copy.wait_send()
 
 
 def per_device(
@@ -689,9 +764,12 @@
             pltpu.VMEM((N, lm, ln), f32),
             pltpu.VMEM((2, lm // 2, ln), f32),
             pltpu.VMEM((2, lm, ln), f32),
-            pltpu.VMEM((GROUPS, N, N, quarter, nc), f32),
-            pltpu.VMEM((GROUPS, 2, N // 2, quarter, nc), f32),
-            pltpu.VMEM((GROUPS, 2, N, quarter, nc), f32),
+            pltpu.VMEM((LAST, N, N, quarter, nc), f32),
+            pltpu.VMEM((LAST, 2, N // 2, quarter, nc), f32),
+            pltpu.VMEM((LAST, 2, N, quarter, nc), f32),
+            pltpu.VMEM((N, N, quarter, nc), f32),
+            pltpu.VMEM((N, 2, quarter // 2, nc), f32),
+            pltpu.VMEM((N, 2, quarter, nc), f32),
             pltpu.VMEM((GROUPS, N, quarter, nc), bf16),
             pltpu.VMEM((col_count, piece, nc), bf16),
             dma((SENDS,)),
@@ -701,7 +779,8 @@
             dma((N,)),
             dma((N, 2)),
             dma((4,)),
-            dma((GROUPS, 4)),
+            dma((LAST, 4)),
+            dma((N, 4)),
             dma((col_count,)),
             dma((5,)),
         ],

time: 126 us -> 122 us (0.968); the launches traced: 126 us -> 120 us
  Pallas kernels: 124 us -> 118 us
    pallas_call x1, Pallas kernels: 124 us -> 118 us  [per_device(): pl.pallas_call(functools.partial(kernel, tile * tile), out_shape=jax.Shap...]
where the time goes in v5:
time: 122 us; the launch traced here: 120 us
  Pallas kernels  118 us (97%)
  local copies, waits for them, and re-layouts  2.06 us (2%)
    pallas_call x1, Pallas kernels, per_device(): pl.pallas_call(functools.partial(kernel, tile * tile), out_shape=jax.Shap...  118 us

profile of v5, /device:TPU:7, one launch (start us, length us, event | category | flops | bytes accessed | tf_op | source)
XLA Modules:
  0.0 120.4 jit_solution(4059499242588547681)
XLA Ops:
  0.0 118.3 %shard_map.100 = f32[1536,128]{1,0:T(8,128)} custom-call(bf16[10,32,1024]{2,1,0:T(8,128)(2,1)} %bitcast.3, bf16[1536,256]{1,0:T(8,128)(2,1)} %la_hbm.1, bf16[2048,128]{1,0:T(8,128)(2,1)} %lb_hbm.1, bf16[5120,384]{1,0:T(8,128)(2,1)} %cb_hbm.1, s32[2,8]{1,0:T(2,128)} %bitcast.4, s32[2,32]{1,0:T(2,128)} %bitcast.5, f32[8]{0:T(128)} %occupied_i.1, ...), custom_call_target="tpu_custom_call" | custom-call | flops 11274289152 | bytes 8388608 | tf_op jit(solution)/shard_map/pallas_call | solution.py:746
  118.3 2.1 %copy.12 = f32[1536,128]{1,0:T(8,128)} copy(f32[1536,128]{1,0:T(8,128)} %shard_map.100) | data formatting | bytes 1572864

commit v6 on v5

--- a/solution.py
+++ b/solution.py
@@ -95,10 +95,11 @@
     def greet(other):
         pl.semaphore_signal(barrier, inc=1, device_id=other, device_id_type=MESH)
 
-    for step in range(1, 8 * N):
-        greet((y, lax.rem(col + step, 8 * N)))
     for step in range(1, N):
-        greet((wrap(y + step), col))
+        greet(device(wrap(y + step), z, x, c))
+        greet(device(y, wrap(z + step), x, c))
+        greet(device(y, z, wrap(x + step), c))
+    greet(sibling)
 
     local_k, blocks, lanes = amps.shape[0], amps.shape[1] // 8, 128
     low = lax.broadcasted_iota(jnp.int32, (1, lanes), 1) < lanes // 2
@@ -158,7 +159,7 @@
         for j in range(occupied_j.shape[0]):
             gaps[j] = virtual - (occupied + occupied_j[j])
 
-    pl.semaphore_wait(barrier, 8 * N + N - 2)
+    pl.semaphore_wait(barrier, 3 * (N - 1) + 1)
 
     started = []
 

time: 122 us -> 119 us (0.975)
  Pallas kernels: 118 us -> 115 us
    pallas_call x1, Pallas kernels: 118 us -> 115 us  [per_device(): pl.pallas_call(functools.partial(kernel, tile * tile), out_shape=jax.Shap...]
where the time goes in v6:
time: 119 us; the launch traced here: 117 us
  Pallas kernels  115 us (97%)
  local copies, waits for them, and re-layouts  2.06 us (2%)
    pallas_call x1, Pallas kernels, per_device(): pl.pallas_call(functools.partial(kernel, tile * tile), out_shape=jax.Shap...  115 us

profile of v6, /device:TPU:7, one launch (start us, length us, event | category | flops | bytes accessed | tf_op | source)
XLA Modules:
  0.0 117.1 jit_solution(4053265915734935844)
XLA Ops:
  0.0 115.0 %shard_map.100 = f32[1536,128]{1,0:T(8,128)} custom-call(bf16[10,32,1024]{2,1,0:T(8,128)(2,1)} %bitcast.3, bf16[1536,256]{1,0:T(8,128)(2,1)} %la_hbm.1, bf16[2048,128]{1,0:T(8,128)(2,1)} %lb_hbm.1, bf16[5120,384]{1,0:T(8,128)(2,1)} %cb_hbm.1, s32[2,8]{1,0:T(2,128)} %bitcast.4, s32[2,32]{1,0:T(2,128)} %bitcast.5, f32[8]{0:T(128)} %occupied_i.1, ...), custom_call_target="tpu_custom_call" | custom-call | flops 11274289152 | bytes 8388608 | tf_op jit(solution)/shard_map/pallas_call | solution.py:747
  115.0 2.1 %copy.12 = f32[1536,128]{1,0:T(8,128)} copy(f32[1536,128]{1,0:T(8,128)} %shard_map.100) | data formatting | bytes 1572864

commit v7 on v6

--- a/solution.py
+++ b/solution.py
@@ -9,7 +9,7 @@
 
 MESH = pl.DeviceIdType.MESH
 N = 4
-SENDS = 304
+SENDS = 96
 GROUPS = 4
 LAST = GROUPS - 1
 
@@ -55,9 +55,13 @@
     outb,
     fin,
     send_sem,
+    sent,
     middle_sem,
+    t_sem,
     a_sem,
+    share_sem,
     la_sem,
+    la_share_sem,
     lx_sem,
     lb_sem,
     lc_sem,
@@ -163,17 +167,18 @@
 
     started = []
 
-    def send(src, dst, sem, other):
+    def send(src, dst, sem, other, done=None):
         copy = pltpu.make_async_remote_copy(
             src_ref=src,
             dst_ref=dst,
-            send_sem=send_sem.at[len(started)],
+            send_sem=send_sem.at[len(started)] if done is None else done,
             recv_sem=sem,
             device_id=other,
             device_id_type=MESH,
         )
         copy.start()
-        started.append(copy)
+        if done is None:
+            started.append(copy)
 
     def arrived(dst, sem):
         pltpu.make_async_remote_copy(
@@ -187,43 +192,45 @@
 
     def a_slot(zz, xx, g, h=None):
         if h is None:
-            return a_buf.at[zz, xx, c, pl.ds(g * group, group)], a_sem.at[zz, xx, c, g, 0]
-        return a_buf.at[zz, xx, c, pl.ds(g * group + h * half, half)], a_sem.at[zz, xx, c, g, h]
+            return a_buf.at[zz, xx, c, pl.ds(g * group, group)]
+        return a_buf.at[zz, xx, c, pl.ds(g * group + h * half, half)]
 
     la_half = la_ref.shape[0] // 2
 
-    def la_slot(zz, core, h=None):
+    def la_slot(zz, h=None):
         if h is None:
-            return la_buf.at[zz, core], la_sem.at[zz, core, 0]
-        return la_buf.at[zz, core, pl.ds(h * la_half, la_half)], la_sem.at[zz, core, h]
+            return la_buf.at[zz, c]
+        return la_buf.at[zz, c, pl.ds(h * la_half, la_half)]
 
     lb_rows = lb_buf.shape[1]
     lb_half = lb_rows // 2
 
-    def lb_slot(yy, h):
-        return lb_buf.at[yy, pl.ds(h * lb_half, lb_half)], lb_sem.at[yy, h]
-
-    def ring_start(slot, at, plus, minus):
-        for h, other in ((0, plus), (1, minus), (1, plus), (0, minus)):
-            ref, sem = slot(at, h)
-            send(ref, ref, sem, other)
-
-    def ring_forward(slot, at, plus, minus):
+    def lb_slot(yy, h=None):
+        if h is None:
+            return lb_buf.at[yy]
+        return lb_buf.at[yy, pl.ds(h * lb_half, lb_half)]
+
+    def ring_piece(slot, sems, at, h, other, sem, done):
+        ref = slot(at, h)
+        send(ref, ref, sems.at[sem], other, done)
+
+    def ring_start(slot, sems, done, at, plus, minus):
+        for h, other, sem in ((0, plus, 0), (1, minus, 1), (1, plus, 2), (0, minus, 2)):
+            ring_piece(slot, sems, at, h, other, sem, done)
+
+    def ring_forward(slot, sems, done, at, plus, minus):
         for h, source, other in ((0, wrap(at - 1), plus), (1, wrap(at + 1), minus)):
-            ref, sem = slot(source, h)
-            arrived(ref, sem)
-            send(ref, ref, sem, other)
-
-    def ring_near(slot, at):
-        arrived(*slot(wrap(at - 1), 1))
-        arrived(*slot(wrap(at + 1), 0))
-
-    def ring_far(slot, at):
-        for h in range(2):
-            arrived(*slot(wrap(at + 2), h))
-
-    def share(ref, sem):
-        send(ref, ref, sem, sibling)
+            arrived(slot(source, h), sems.at[h])
+            ring_piece(slot, sems, source, h, other, 3, done)
+
+    def ring_near(slot, sems, at):
+        arrived(slot(wrap(at - 1)), sems.at[2])
+
+    def ring_far(slot, sems, at):
+        arrived(slot(wrap(at + 2)), sems.at[3])
+
+    def share(ref, sem, done):
+        send(ref, ref, sem, sibling, done)
 
     z_plus, z_minus = device(y, wrap(z + 1), x, c), device(y, wrap(z - 1), x, c)
     x_plus, x_minus = device(y, z, wrap(x + 1), c), device(y, z, wrap(x - 1), c)
@@ -253,7 +260,7 @@
             src_ref=ref.at[part],
             dst_ref=a_buf.at[z, x, c, part],
             send_sem=send_sem.at[SENDS - 1 - 2 * GROUPS - 2 * g - h],
-            recv_sem=a_sem.at[z, x, c, g, h],
+            recv_sem=t_sem.at[g, h],
             device_id=(swapped(g), col),
             device_id_type=MESH,
         )
@@ -315,39 +322,41 @@
         local_sem.at[4],
     )
 
-    def la_own(p, h=None):
-        return la_slot(p, c, h)
+    la_ring = z, z_plus, z_minus
+
+    def la_share(zz):
+        share(la_slot(zz), la_share_sem.at[0], sent.at[2])
 
     def la_start():
         screen_amps()
-        ring_start(la_own, z, z_plus, z_minus)
-        share(*la_slot(z, c))
+        ring_start(la_slot, la_sem, sent.at[2], *la_ring)
+        la_share(z)
 
     def la_forward():
-        ring_forward(la_own, z, z_plus, z_minus)
+        ring_forward(la_slot, la_sem, sent.at[2], *la_ring)
 
     def la_near():
-        ring_near(la_own, z)
-        for q in (wrap(z - 1), wrap(z + 1)):
-            share(*la_slot(q, c))
+        ring_near(la_slot, la_sem, z)
+        la_share(wrap(z - 1))
+        la_share(wrap(z + 1))
 
     def la_far():
-        ring_far(la_own, z)
-        share(*la_slot(wrap(z + 2), c))
+        ring_far(la_slot, la_sem, z)
+        la_share(wrap(z + 2))
 
     def lb_start():
         keep_lb.wait()
         for step in range(1, N):
             source = wrap(x + step)
             arrived(lb_buf.at[y, :, pl.ds(pl.multiple_of(source * width, width), width)], lx_sem.at[source])
-        ring_start(lb_slot, y, y_plus, y_minus)
+        ring_start(lb_slot, lb_sem, None, y, y_plus, y_minus)
 
     def lb_forward():
-        ring_forward(lb_slot, y, y_plus, y_minus)
+        ring_forward(lb_slot, lb_sem, None, y, y_plus, y_minus)
 
     def lb_end():
-        ring_near(lb_slot, y)
-        ring_far(lb_slot, y)
+        ring_near(lb_slot, lb_sem, y)
+        ring_far(lb_slot, lb_sem, y)
 
     z_first = axis_order(c)
 
@@ -359,59 +368,69 @@
 
     def first(g):
         f = z_first[g]
-        return (lambda q, h=None: a_slot(f * q + (1 - f) * z, f * x + (1 - f) * q, g, h)), ring_of(f)
+
+        def slot(q, h=None):
+            return a_slot(f * q + (1 - f) * z, f * x + (1 - f) * q, g, h)
+
+        return slot, a_sem.at[g, 0], ring_of(f)
 
     def second(g, k):
         f = z_first[g]
         p = wrap(f * z + (1 - f) * x + (0, 3, 1, 2)[k]) if g < LAST else swapped(g, k)
-        return (lambda q, h=None: a_slot(f * p + (1 - f) * q, f * q + (1 - f) * p, g, h)), ring_of(1 - f)
+
+        def slot(q, h=None):
+            return a_slot(f * p + (1 - f) * q, f * q + (1 - f) * p, g, h)
+
+        return slot, a_sem.at[g, 1 + k], ring_of(1 - f)
+
+    def a_share(slot, at, g, k):
+        share(slot(at), share_sem.at[g if g < LAST else LAST + k], sent.at[1])
 
     def second_start(g, k):
-        slot, ring = second(g, k)
-        ring_start(slot, *ring)
-        share(*slot(ring[0]))
+        slot, sems, ring = second(g, k)
+        ring_start(slot, sems, sent.at[0], *ring)
+        a_share(slot, ring[0], g, k)
 
     def second_forward(g, k):
-        slot, ring = second(g, k)
-        ring_forward(slot, *ring)
+        slot, sems, ring = second(g, k)
+        ring_forward(slot, sems, sent.at[0], *ring)
 
     def second_near(g, k):
-        slot, ring = second(g, k)
-        ring_near(slot, ring[0])
+        slot, sems, ring = second(g, k)
+        ring_near(slot, sems, ring[0])
         for p in (wrap(ring[0] - 1), wrap(ring[0] + 1)):
-            share(*slot(p))
+            a_share(slot, p, g, k)
 
     def second_far(g, k):
-        slot, ring = second(g, k)
-        ring_far(slot, ring[0])
-        share(*slot(wrap(ring[0] + 2)))
+        slot, sems, ring = second(g, k)
+        ring_far(slot, sems, ring[0])
+        a_share(slot, wrap(ring[0] + 2), g, k)
 
     def first_start(g):
-        near = (first(g), second(g, 0)) if g < LAST else (first(g),)
+        both = (first(g), second(g, 0)) if g < LAST else (first(g),)
         for h in range(2):
             end_over_y(g, h)
-            for slot, (at, plus, minus) in near:
-                ref, sem = slot(at, h)
-                for other in (plus, minus) if h == 0 else (minus, plus):
-                    send(ref, ref, sem, other)
+            for slot, sems, (at, plus, minus) in both:
+                for other, sem in ((plus, 0), (minus, 2)) if h == 0 else ((minus, 1), (plus, 2)):
+                    ring_piece(slot, sems, at, h, other, sem, sent.at[0])
         if g < LAST:
-            slot, ring = near[1]
-            share(*slot(ring[0]))
+            slot, _, ring = both[1]
+            a_share(slot, ring[0], g, 0)
 
     def first_forward(g):
-        slot, ring = first(g)
-        ring_forward(slot, *ring)
+        slot, sems, ring = first(g)
+        ring_forward(slot, sems, sent.at[0], *ring)
 
     def first_near(g):
-        slot, ring = first(g)
-        ring_near(slot, ring[0])
+        slot, sems, ring = first(g)
+        ring_near(slot, sems, ring[0])
         if g < LAST:
             second_start(g, 1)
             second_start(g, 2)
 
     def first_far(g):
-        slot, ring = first(g)
-        ring_far(slot, ring[0])
+        slot, sems, ring = first(g)
+        ring_far(slot, sems, ring[0])
         if g < LAST:
             second_start(g, 3)
 
@@ -419,8 +438,7 @@
     lk = la_ref.shape[1]
 
     def ladder():
-        for step in range(N):
-            arrived(*la_slot(wrap(z + step), 1 - c))
+        arrived(la_buf.at[:, 1 - c], la_share_sem.at[0])
 
         @pl.loop(0, la_ref.shape[0] // tile)
         def _(m):
@@ -469,9 +487,7 @@
     mine = x * 2 + c
 
     def cycle(g):
-        for zz in range(N):
-            for xx in range(N):
-                arrived(a_buf.at[zz, xx, 1 - c, group_rows(g)], a_sem.at[zz, xx, 1 - c, g, 0])
+        arrived(a_buf.at[:, :, 1 - c, group_rows(g)], share_sem.at[g])
         total = jnp.zeros((rows // GROUPS * N, cb_ref.shape[1]), jnp.float32)
         for xx in range(N):
             for core in range(2):
@@ -496,7 +512,7 @@
             src_ref=outb.at[g, z, pl.ds(pl.multiple_of(turn * piece, piece), piece)],
             dst_ref=fin.at[col],
             send_sem=send_sem.at[SENDS - 1 - 4 * GROUPS - g],
-            recv_sem=fin_sem.at[col],
+            recv_sem=fin_sem.at[0],
             device_id=(y, z * 8 + g * pairs + turn),
             device_id_type=MESH,
         )
@@ -512,7 +528,7 @@
                 send(
                     outb.at[g, zz, pl.ds(pl.multiple_of(turn * piece, piece), piece)],
                     fin.at[col],
-                    fin_sem.at[col],
+                    fin_sem.at[0],
                     (y, zz * 8 + g * pairs + turn),
                 )
 
@@ -526,8 +542,7 @@
 
     def block(k):
         zz = swapped(LAST, k)
-        for xx in range(N):
-            arrived(a_buf.at[zz, xx, 1 - c, group_rows(LAST)], a_sem.at[zz, xx, 1 - c, LAST, 0])
+        arrived(a_buf.at[zz, :, 1 - c, group_rows(LAST)], share_sem.at[LAST + k])
         total = jnp.zeros((group, cb_ref.shape[1]), jnp.float32)
         for xx in range(N):
             for core in range(2):
@@ -549,7 +564,7 @@
             src_ref=outb.at[LAST, k, pl.ds(n * piece, piece)],
             dst_ref=fin.at[col],
             send_sem=send_sem.at[SENDS - 1 - 5 * GROUPS - pairs * k - n],
-            recv_sem=fin_sem.at[col],
+            recv_sem=fin_sem.at[0],
             device_id=(y, other),
             device_id_type=MESH,
         )
@@ -679,9 +694,7 @@
     block_end(2)
     ladder_end()
 
-    for step in range(1, 8 * N):
-        source = lax.rem(col + step, 8 * N)
-        arrived(fin.at[source], fin_sem.at[source])
+    arrived(fin.at[pl.ds(0, 8 * N - 1)], fin_sem.at[0])
 
     @pl.loop(0, 8 * N, unroll=4)
     def _(source):
@@ -691,6 +704,18 @@
                 j = source * (fin.shape[2] // lanes * 2) + 2 * m + n
                 out_ref[pl.ds(j, 8, stride=pair_count), :] = (ladder_ji[j] + value) / gaps[j]
 
+    ring_rows = GROUPS * 6 * (1 + N) * half // (2 * N * N)
+    share_rows = GROUPS * N * N * group // (2 * N * N)
+    la_rows = (6 + 2 * N) * la_half // (2 * N)
+    for n, ref in enumerate((a_buf.at[:, :, :, :ring_rows], a_buf.at[:, :, :, :share_rows], la_buf.at[:, :, :la_rows])):
+        pltpu.make_async_remote_copy(
+            src_ref=ref,
+            dst_ref=ref,
+            send_sem=sent.at[n],
+            recv_sem=fin_sem.at[0],
+            device_id=sibling,
+            device_id_type=MESH,
+        ).wait_send()
     for copy in started:
         copy.wait_send()
     for g in range(GROUPS):
@@ -774,15 +799,19 @@
             pltpu.VMEM((GROUPS, N, quarter, nc), bf16),
             pltpu.VMEM((col_count, piece, nc), bf16),
             dma((SENDS,)),
+            dma((3,)),
             dma((GROUPS, 2)),
-            dma((N, N, 2, GROUPS, 2)),
-            dma((N, 2, 2)),
+            dma((GROUPS, 2)),
+            dma((GROUPS, 1 + N, 4)),
+            dma((LAST + N,)),
+            dma((4,)),
+            dma((1,)),
             dma((N,)),
-            dma((N, 2)),
+            dma((4,)),
             dma((4,)),
             dma((LAST, 4)),
             dma((N, 4)),
-            dma((col_count,)),
+            dma((1,)),
             dma((5,)),
         ],
         compiler_params=pltpu.CompilerParams(

time: 119 us -> 115 us (0.966)
  Pallas kernels: 115 us -> 111 us
    pallas_call x1, Pallas kernels: 115 us -> 111 us  [per_device(): pl.pallas_call(functools.partial(kernel, tile * tile), out_shape=jax.Shap...]
where the time goes in v7:
time: 115 us; the launch traced here: 113 us
  Pallas kernels  111 us (97%)
  local copies, waits for them, and re-layouts  2.06 us (2%)
    pallas_call x1, Pallas kernels, per_device(): pl.pallas_call(functools.partial(kernel, tile * tile), out_shape=jax.Shap...  111 us

profile of v7, /device:TPU:7, one launch (start us, length us, event | category | flops | bytes accessed | tf_op | source)
XLA Modules:
  0.0 113.2 jit_solution(12413387183296430765)
XLA Ops:
  0.0 111.1 %shard_map.100 = f32[1536,128]{1,0:T(8,128)} custom-call(bf16[10,32,1024]{2,1,0:T(8,128)(2,1)} %bitcast.3, bf16[1536,256]{1,0:T(8,128)(2,1)} %la_hbm.1, bf16[2048,128]{1,0:T(8,128)(2,1)} %lb_hbm.1, bf16[5120,384]{1,0:T(8,128)(2,1)} %cb_hbm.1, s32[2,8]{1,0:T(2,128)} %bitcast.4, s32[2,32]{1,0:T(2,128)} %bitcast.5, f32[8]{0:T(128)} %occupied_i.1, ...), custom_call_target="tpu_custom_call" | custom-call | flops 11274289152 | bytes 8388608 | tf_op jit(solution)/shard_map/pallas_call | solution.py:772
  111.1 2.1 %copy.12 = f32[1536,128]{1,0:T(8,128)} copy(f32[1536,128]{1,0:T(8,128)} %shard_map.100) | data formatting | bytes 1572864

commit v8 on v7

--- a/solution.py
+++ b/solution.py
@@ -30,6 +30,7 @@
     occupied_j,
     virtual_a,
     virtual_b,
+    out_any,
     out_ref,
     amps,
     screened,
@@ -460,7 +461,7 @@
         reduce_middle(lc, lc_a, lc_b, lc_sem, x, x_plus, x_minus)
 
     def ladder_end():
-        out_ref[...] = reduce_end(lc, lc_b, lc_sem, x)
+        out_ref[pl.ds(0, out_any.shape[0]), :] = reduce_end(lc, lc_b, lc_sem, x)
         for j in range(pair_count):
             ladder_ji[j] = out_ref[pl.ds(j, 8, stride=pair_count), :]
 
@@ -704,6 +705,9 @@
                 j = source * (fin.shape[2] // lanes * 2) + 2 * m + n
                 out_ref[pl.ds(j, 8, stride=pair_count), :] = (ladder_ji[j] + value) / gaps[j]
 
+    result = pltpu.make_async_copy(out_ref.at[pl.ds(0, out_any.shape[0])], out_any, local_sem.at[5])
+    result.start()
+
     ring_rows = GROUPS * 6 * (1 + N) * half // (2 * N * N)
     share_rows = GROUPS * N * N * group // (2 * N * N)
     la_rows = (6 + 2 * N) * la_half // (2 * N)
@@ -718,6 +722,7 @@
         ).wait_send()
     for copy in started:
         copy.wait_send()
+    result.wait()
     for g in range(GROUPS):
 
         @pl.when(y != 2 * (g % 2))
@@ -773,8 +778,9 @@
         functools.partial(kernel, tile * tile),
         out_shape=jax.ShapeDtypeStruct((lm, ln), f32),
         in_specs=[hbm] * 4 + [smem] * 6,
-        out_specs=pl.BlockSpec(memory_space=pltpu.VMEM),
+        out_specs=hbm,
         scratch_shapes=[
+            pltpu.VMEM((lm + occupied_j.shape[0], ln), f32),
             pltpu.VMEM((local_k, all_i, ac), bf16),
             pltpu.VMEM((lrows, ln), bf16),
             pltpu.VMEM((occupied_j.shape[0], occupied_i.shape[0], ln), f32),
@@ -812,7 +818,7 @@
             dma((LAST, 4)),
             dma((N, 4)),
             dma((1,)),
-            dma((5,)),
+            dma((6,)),
         ],
         compiler_params=pltpu.CompilerParams(
             collective_id=0, has_side_effects=True, vmem_limit_bytes=56 * 2**20

time: 115 us -> 115 us (level)
  no operation moved by 1% of the time
where the time goes in v8:
time: 115 us; the launch traced here: 113 us
  Pallas kernels  111 us (97%)
  local copies, waits for them, and re-layouts  2.06 us (2%)
    pallas_call x1, Pallas kernels, per_device(): pl.pallas_call(functools.partial(kernel, tile * tile), out_shape=jax.Shap...  111 us

profile of v8, /device:TPU:7, one launch (start us, length us, event | category | flops | bytes accessed | tf_op | source)
XLA Modules:
  0.0 113.1 jit_solution(8729228384533942918)
XLA Ops:
  0.0 111.0 %shard_map.100 = f32[1536,128]{1,0:T(8,128)} custom-call(bf16[10,32,1024]{2,1,0:T(8,128)(2,1)} %bitcast.3, bf16[1536,256]{1,0:T(8,128)(2,1)} %la_hbm.1, bf16[2048,128]{1,0:T(8,128)(2,1)} %lb_hbm.1, bf16[5120,384]{1,0:T(8,128)(2,1)} %cb_hbm.1, s32[2,8]{1,0:T(2,128)} %bitcast.4, s32[2,32]{1,0:T(2,128)} %bitcast.5, f32[8]{0:T(128)} %occupied_i.1, ...), custom_call_target="tpu_custom_call" | custom-call | flops 11274289152 | bytes 8388608 | tf_op jit(solution)/shard_map/pallas_call | solution.py:777
  111.0 2.1 %copy.12 = f32[1536,128]{1,0:T(8,128)} copy(f32[1536,128]{1,0:T(8,128)} %shard_map.100) | data formatting | bytes 1572864
